TPU v7x, 128 devices: a whole 4x4x4 slice. The times are simulated.
128 devices in a mesh: sample: 2 (over x_lo), row: 8 (over y, core), col: 8 (over z, x_hi).
Axes of the slice: x: 4 (x_hi: 2, x_lo: 2; x = x_hi * 2 + x_lo), y: 4, z: 4, core: 2. Of those that a mesh axis runs over, the one named last changes fastest.
Arguments:
- images: bfloat16 [2, 512, 32768], P('sample', 'row', 'col'), may hold values from -6 to 6
- first_weight: bfloat16 [576, 128], replicated, may hold values from -0.25 to 0.25
- deep_weight: bfloat16 [1152, 256], P(None, 'col'), may hold values from -0.1875 to 0.1875
- deep_cotangent: bfloat16 [2, 256, 128, 128], P('sample', 'col', 'row'), may hold values from -0.046875 to 0.046875
Outputs:
- first_grad_weight: float32 [576, 128], replicated
- deep_grad_weight: float32 [1152, 256], P('row', 'col')
All inputs are finite; a program needn't handle non-finite values.
Results may differ from a plain program's by a relative error of at most 0.0059.
Values may be sent and summed in bfloat16 or wider, within the bound.
A program may use at most 64 MiB of HBM per device.

v0:
```python
import jax
import jax.numpy as jnp
from jax import lax
from jax.sharding import PartitionSpec as P

C0 = 64
C1 = 128


def from_behind(value, axis, steps):
    count = lax.axis_size(axis)
    initial, last = (max(0, -steps), min(count, count - steps))
    return lax.ppermute(value, axis, [(source, source + steps) for source in range(initial, last)])


def taps_of(padded, out_rows, out_cols):
    pieces = []
    for row_off in range(3):
        for col_off in range(3):
            pieces.append(
                padded[
                    :, row_off : row_off + 2 * out_rows : 2, col_off : col_off + 2 * out_cols : 2
                ]
            )
    return jnp.stack(pieces, 1)


def extended_matrix(extended):
    channels = extended.shape[0]
    return taps_of(extended, (extended.shape[1] - 1) // 2, (extended.shape[2] - 1) // 2).reshape(
        channels * 9, -1
    )


def silu_slope(value):
    logistic = jax.nn.sigmoid(value)
    return logistic * (1.0 + value * (1.0 - logistic))


def on_device(images, first_weight, deep_weight, deep_cotangent):
    n_cols = lax.axis_size("col")
    tile_rows = images.shape[1]
    tile_cols = images.shape[2] // C0
    tile_in = images[0].reshape(tile_rows, tile_cols, C0).transpose(2, 0, 1)
    half = tile_rows // 2
    quarter = half // 2
    shard_out = deep_weight.shape[1]
    above = from_behind(tile_in[:, -1:, :], "row", 1)
    extended = jnp.concatenate([above, tile_in], 1)
    leftside = from_behind(extended[:, :, -1:], "col", 1)
    extended = jnp.concatenate([leftside, extended], 2)
    first_patches = extended_matrix(extended)
    first_pre = jnp.dot(first_weight.T, first_patches, preferred_element_type=jnp.float32)
    first_pre = first_pre.reshape(C1, half, half)
    first_act = jax.nn.silu(first_pre).astype(jnp.bfloat16)
    strip = lax.all_gather(first_act, "col", axis=2, tiled=True)
    strip_top = from_behind(strip[:, -1:, :], "row", 1)
    strip_ext = jnp.concatenate([strip_top, strip], 1)
    strip_ext = jnp.pad(strip_ext, ((0, 0), (0, 0), (1, 0)))
    out_cols = n_cols * quarter
    kernel_taps = deep_weight.reshape(C1, 9, shard_out)
    deep_pre = jnp.zeros((shard_out, quarter * out_cols), jnp.float32)
    for row_off in range(3):
        for col_off in range(3):
            view = strip_ext[
                :, row_off : row_off + 2 * quarter : 2, col_off : col_off + 2 * out_cols : 2
            ].reshape(C1, -1)
            deep_pre = deep_pre + jnp.dot(
                kernel_taps[:, 3 * row_off + col_off, :].T, view, preferred_element_type=jnp.float32
            )
    cot_strip = deep_cotangent[0].reshape(shard_out, -1).astype(jnp.float32)
    deep_grad = (cot_strip * silu_slope(deep_pre)).astype(jnp.bfloat16)
    kernel_parts = []
    ext_grad = jnp.zeros(strip_ext.shape, jnp.float32)
    for row_off in range(3):
        for col_off in range(3):
            view = strip_ext[
                :, row_off : row_off + 2 * quarter : 2, col_off : col_off + 2 * out_cols : 2
            ].reshape(C1, -1)
            kernel_parts.append(jnp.dot(view, deep_grad.T, preferred_element_type=jnp.float32))
            contrib = jnp.dot(
                kernel_taps[:, 3 * row_off + col_off, :],
                deep_grad,
                preferred_element_type=jnp.float32,
            )
            ext_grad = ext_grad.at[
                :, row_off : row_off + 2 * quarter : 2, col_off : col_off + 2 * out_cols : 2
            ].add(contrib.reshape(C1, quarter, out_cols))
    kernel_local = jnp.stack(kernel_parts, 1).reshape(C1 * 9, shard_out)
    deep_local = lax.psum_scatter(kernel_local, "row", scatter_dimension=0, tiled=True)
    terms = ext_grad[:, :, 1:]
    own_cols = lax.psum_scatter(terms, "col", scatter_dimension=2, tiled=True)
    from_below = from_behind(own_cols[:, :1, :], "row", -1)
    tile_grad = own_cols[:, 1:, :]
    tile_grad = jnp.concatenate([tile_grad[:, :-1, :], tile_grad[:, -1:, :] + from_below], 1)
    act_grad = tile_grad.astype(jnp.bfloat16)
    deep_total = lax.psum(deep_local, "sample")
    first_grad = (act_grad.astype(jnp.float32) * silu_slope(first_pre)).astype(jnp.bfloat16)
    first_local = jnp.dot(
        first_patches, first_grad.reshape(C1, -1).T, preferred_element_type=jnp.float32
    )
    first_total = lax.psum(first_local, ("sample", "row", "col"))
    return (first_total, deep_total)


def solution(mesh):
    return jax.shard_map(
        on_device,
        mesh=mesh,
        in_specs=(P("sample", "row", "col"), P(), P(None, "col"), P("sample", "col", "row", None)),
        out_specs=(P(), P("row", "col")),
        check_vma=False,
    )
```

profile of v0, /device:TPU:1, one launch (start us, length us, event | category | flops | bytes accessed | tf_op | source)
XLA Modules:
  0.0 639.0 jit_solution(7599031088975900379)
XLA Ops:
  24.0 9.9 %slice.127 = bf16[64,32,32]{0,2,1:T(8,128)(2,1)} slice(bf16[64,65,64]{0,2,1:T(8,128)(2,1)S(1)} %pad_maximum_fusion), slice={[0:64:1], [0:64:2], [0:64:2]} | slice | bytes 262144 | tf_op jit(solution)/shard_map/slice | solution.py:21
  33.8 9.8 %slice.128 = bf16[64,32,32]{0,2,1:T(8,128)(2,1)} slice(bf16[64,65,64]{0,2,1:T(8,128)(2,1)S(1)} %pad_maximum_fusion), slice={[0:64:1], [0:64:2], [1:64:2]} | slice | bytes 262144 | tf_op jit(solution)/shard_map/slice | solution.py:21
  44.2 9.9 %slice.126 = bf16[64,32,32]{0,2,1:T(8,128)(2,1)} slice(bf16[64,65,65]{0,2,1:T(8,128)(2,1)S(1)} %maximum_maximum_fusion), slice={[0:64:1], [0:64:2], [0:64:2]} | slice | bytes 262144 | tf_op jit(solution)/shard_map/slice | solution.py:21
  54.1 9.8 %slice.129 = bf16[64,32,32]{0,2,1:T(8,128)(2,1)} slice(bf16[64,65,65]{0,2,1:T(8,128)(2,1)S(1)} %maximum_maximum_fusion), slice={[0:64:1], [1:65:2], [0:64:2]} | slice | bytes 262144 | tf_op jit(solution)/shard_map/slice | solution.py:21
  63.9 9.9 %slice.132 = bf16[64,32,32]{0,2,1:T(8,128)(2,1)} slice(bf16[64,65,65]{0,2,1:T(8,128)(2,1)S(1)} %maximum_maximum_fusion), slice={[0:64:1], [2:65:2], [0:64:2]} | slice | bytes 262144 | tf_op jit(solution)/shard_map/slice | solution.py:21
  78.1 8.5 %copy.60 = bf16[64,9,32,32]{3,2,1,0:T(8,128)(2,1)} copy(bf16[64,9,32,32]{0,3,2,1:T(8,128)(2,1)S(1)} %bitcast_dynamic-update-slice_fusion) | data formatting | bytes 2359296 | tf_op jit(solution)/shard_map/stack | solution.py:25
  86.5 6.8 %reshape.86 = bf16[576,1024]{1,0:T(8,128)(2,1)S(1)} reshape(bf16[64,9,32,32]{3,2,1,0:T(8,128)(2,1)} %copy.60) | data formatting | bytes 2359296 | tf_op jit(solution)/shard_map/reshape | solution.py:30
  97.5 52.3 %all-gather.2.cloned.1.call-done = bf16[128,32,256]{0,2,1:T(8,128)(2,1)} async-done(((bf16[128,32,32]{0,2,1:T(8,128)(2,1)}), bf16[128,32,256]{0,2,1:T(8,128)(2,1)}) %all-gather.2.cloned.1.call-update) | async-done | bytes 2097168 | tf_op jit(solution)/shard_map/all_gather | solution.py:56
  190.2 5.4 slice.148
  196.7 5.5 slice.152
  220.1 14.1 %scatter_custom_fusion = f32[8481,128]{1,0:T(8,128)} fusion(s32[2048]{0:T(1024)} %select_bitcast_fusion.8, f32[2048,128]{1,0:T(8,128)} %fusion.102, f32[]{:T(128)} %constant.5.clone.1), kind=kCustom, calls=%fused_computation.22 | custom fusion | flops 262144 | bytes 4342784
  234.2 15.0 %scatter_fusion = f32[8481,128]{1,0:T(8,128)} fusion(f32[8481,128]{1,0:T(8,128)} %scatter_custom_fusion, s32[2048]{0:T(1024)S(1)} %copy-done.14, f32[2048,128]{1,0:T(8,128)} %fusion.99), kind=kCustom, calls=%fused_computation.1 | custom fusion | flops 262144 | bytes 3153920
  249.2 15.0 %scatter_fusion.1 = f32[8481,128]{1,0:T(8,128)} fusion(f32[8481,128]{1,0:T(8,128)} %scatter_fusion, s32[2048]{0:T(1024)S(1)} %get-tuple-element.43, f32[2048,128]{1,0:T(8,128)} %fusion.96), kind=kCustom, calls=%fused_computation.2 | custom fusion | flops 262144 | bytes 3153920
  264.2 15.0 %scatter_fusion.2 = f32[8481,128]{1,0:T(8,128)} fusion(f32[8481,128]{1,0:T(8,128)} %scatter_fusion.1, s32[2048]{0:T(1024)S(1)} %copy-done.13, f32[2048,128]{1,0:T(8,128)} %fusion.93), kind=kCustom, calls=%fused_computation.3 | custom fusion | flops 262144 | bytes 3153920
  279.1 15.0 %scatter_fusion.3 = f32[8481,128]{1,0:T(8,128)} fusion(f32[8481,128]{1,0:T(8,128)} %scatter_fusion.2, s32[2048]{0:T(1024)S(1)} %get-tuple-element.41, f32[2048,128]{1,0:T(8,128)} %fusion.90), kind=kCustom, calls=%fused_computation.4 | custom fusion | flops 262144 | bytes 3153920
  294.1 15.0 %scatter_fusion.4 = f32[8481,128]{1,0:T(8,128)} fusion(f32[8481,128]{1,0:T(8,128)} %scatter_fusion.3, s32[2048]{0:T(1024)S(1)} %get-tuple-element.40, f32[2048,128]{1,0:T(8,128)} %fusion.87), kind=kCustom, calls=%fused_computation.5 | custom fusion | flops 262144 | bytes 3153920
  309.1 15.0 %scatter_fusion.5 = f32[8481,128]{1,0:T(8,128)} fusion(f32[8481,128]{1,0:T(8,128)} %scatter_fusion.4, s32[2048]{0:T(1024)S(1)} %get-tuple-element.39, f32[2048,128]{1,0:T(8,128)} %fusion.84), kind=kCustom, calls=%fused_computation.6 | custom fusion | flops 262144 | bytes 3153920
  324.0 15.0 %scatter_fusion.6 = f32[8481,128]{1,0:T(8,128)} fusion(f32[8481,128]{1,0:T(8,128)} %scatter_fusion.5, s32[2048]{0:T(1024)S(1)} %get-tuple-element.38, f32[2048,128]{1,0:T(8,128)} %fusion.81), kind=kCustom, calls=%fused_computation.7 | custom fusion | flops 262144 | bytes 3153920
  339.0 15.0 %scatter_fusion.7 = f32[8481,128]{1,0:T(8,128)} fusion(f32[8481,128]{1,0:T(8,128)} %scatter_fusion.6, s32[2048]{0:T(1024)S(1)} %get-tuple-element.37, f32[2048,128]{1,0:T(8,128)} %fusion.78), kind=kCustom, calls=%fused_computation.8 | custom fusion | flops 262144 | bytes 3153920
  353.9 5.2 reshape.142
  373.6 72.7 %reduce-scatter.3.cloned.1.call-done = f32[128,33,32]{0,2,1:T(8,128)} async-done(((f32[128,33,256]{0,2,1:T(8,128)}), f32[128,33,32]{0,2,1:T(8,128)}) %reduce-scatter.3.cloned.1.call-update) | async-done | bytes 540688 | tf_op jit(solution)/shard_map/reduce_scatter | solution.py:92
  456.7 25.0 %reduce-scatter.5.cloned.1.call-done = f32[144,32]{1,0:T(8,128)} async-done(((f32[1152,32]{1,0:T(8,128)}), f32[144,32]{1,0:T(8,128)}) %reduce-scatter.5.cloned.1.call-update) | async-done | bytes 18448 | tf_op jit(solution)/shard_map/reduce_scatter | solution.py:90
  481.7 7.6 %psum.15 = f32[144,32]{1,0:T(8,128)S(1)} all-reduce(f32[144,32]{1,0:T(8,128)} %reduce-scatter.5.cloned.1.call-done), channel_id=1, replica_groups=mesh['sample'=2,'row'=8,'col'=8] {'sample'}, use_global_device_ids=true, to_apply=%region_12.13 | all-reduce | flops 4608 | bytes 36864 | tf_op jit(solution)/shard_map/psum | solution.py:97
  490.0 140.8 %all-reduce.3.cloned.1.call-done = f32[576,128]{1,0:T(8,128)} async-done(((f32[576,128]{1,0:T(8,128)}), f32[576,128]{1,0:T(8,128)}) %all-reduce.3.cloned.1.call-update) | async-done | bytes 294928 | tf_op jit(solution)/shard_map/psum | solution.py:102
  (153 shorter events, 111.9 us)
Async XLA Ops:
  7.2 86.2 %copy-start = (bf16[576,128]{1,0:T(8,128)(2,1)S(1)}, bf16[576,128]{1,0:T(8,128)(2,1)}, u32[]{:S(2)}) copy-start(bf16[576,128]{1,0:T(8,128)(2,1)} %param.5) | copy-start | bytes 442372
  7.2 142.6 %all-gather.2.cloned.1.call-start = ((), (), s32[]{:S(2)}) async-start(), calls=%async_computation.2 | async-start | bytes 2359296 | tf_op jit(solution)/shard_map/all_gather | solution.py:56
  9.4 9.4 %collective-permute-start = (bf16[64,1,64]{2,0,1:T(8,128)(2,1)S(1)}, bf16[64,1,64]{2,0,1:T(8,128)(2,1)S(1)}, u32[]{:S(2)}, u32[]{:S(2)}) collective-permute-start(bf16[64,1,64]{2,0,1:T(8,128)(2,1)S(1)} %copy.56), channel_id=1, source_target_pairs={{0,8},{8,16},{16,24},{24,32},{32,40},{40,48},{48,56},{1,9},{9,17},... | collective-permute-start | bytes 24584 | tf_op jit(solution)/shard_map/ppermute | solution.py:13
  19.1 24.6 %collective-permute-start.1 = (bf16[64,65,1]{1,0,2:T(8,128)(2,1)S(1)}, bf16[64,65,1]{1,0,2:T(8,128)(2,1)S(1)}, u32[]{:S(2)}, u32[]{:S(2)}) collective-permute-start(bf16[64,65,1]{1,0,2:T(8,128)(2,1)S(1)} %copy.58), channel_id=1, source_target_pairs={{0,1},{1,2},{2,3},{3,4},{4,5},{5,6},{6,7},{8,9},{9,10},{10,11},{11... | collective-permute-start | bytes 24968 | tf_op jit(solution)/shard_map/ppermute | solution.py:13
  73.8 4.1 copy-start.8
  93.3 4.1 copy-start.1
  93.3 1.5 copy-start.12
  93.3 2.2 copy-start.16
  93.4 2.3 copy-start.15
  94.0 62.3 %copy-start.11 = (bf16[1,32,16,128]{3,2,1,0:T(8,128)(2,1)S(1)}, bf16[1,32,16,128]{3,2,1,0:T(8,128)(2,1)}, u32[]{:S(2)}) copy-start(bf16[1,32,16,128]{3,2,1,0:T(8,128)(2,1)} %param.7) | copy-start | bytes 393220
  94.8 351.5 %reduce-scatter.3.cloned.1.call-start = ((), (), s32[]{:S(2)}) async-start(), calls=%async_computation.3 | async-start | bytes 4866048 | tf_op jit(solution)/shard_map/reduce_scatter | solution.py:92
  150.6 6.4 %collective-permute-start.2 = (bf16[128,1,256]{0,2,1:T(8,128)(2,1)S(1)}, bf16[128,1,256]{0,2,1:T(8,128)(2,1)S(1)}, u32[]{:S(2)}, u32[]{:S(2)}) collective-permute-start(bf16[128,1,256]{0,2,1:T(8,128)(2,1)S(1)} %slice.161), channel_id=1, source_target_pairs={{0,8},{8,16},{16,24},{24,32},{32,40},{40,48},{48,56},{1,9},{9,17},... | collective-permute-start | bytes 196616 | tf_op jit(solution)/shard_map/ppermute | solution.py:13
  202.2 4.2 copy-start.6
  202.2 4.5 copy-start.5
  202.2 4.8 copy-start.4
  205.0 2.3 copy-start.3
  206.7 1.2 copy-start.7
  220.1 14.1 %copy-start.14 = (s32[2048]{0:T(1024)S(1)}, s32[2048]{0:T(1024)}, u32[]{:S(2)}) copy-start(s32[2048]{0:T(1024)} %get-tuple-element.44) | copy-start | bytes 24580
  249.2 15.0 %copy-start.13 = (s32[2048]{0:T(1024)S(1)}, s32[2048]{0:T(1024)}, u32[]{:S(2)}) copy-start(s32[2048]{0:T(1024)} %get-tuple-element.42) | copy-start | bytes 24580
  363.9 117.8 %reduce-scatter.5.cloned.1.call-start = ((), (), s32[]{:S(2)}) async-start(), calls=%async_computation.5 | async-start | bytes 663552 | tf_op jit(solution)/shard_map/reduce_scatter | solution.py:90
  447.0 8.0 %collective-permute-start.3 = (f32[128,1,32]{0,2,1:T(8,128)S(1)}, f32[128,1,32]{0,2,1:T(8,128)S(1)}, u32[]{:S(2)}, u32[]{:S(2)}) collective-permute-start(f32[128,1,32]{0,2,1:T(8,128)S(1)} %slice.174), channel_id=1, source_target_pairs={{8,0},{16,8},{24,16},{32,24},{40,32},{48,40},{56,48},{9,1},{17,9},... | collective-permute-start | bytes 49160 | tf_op jit(solution)/shard_map/ppermute | solution.py:13
  452.5 2.5 copy-start.10
  454.0 1.5 copy-start.2
  454.9 175.9 %all-reduce.3.cloned.1.call-start = ((), (), s32[]{:S(2)}) async-start(), calls=%async_computation.4 | async-start | bytes 589824 | tf_op jit(solution)/shard_map/psum | solution.py:102
  (1 other events, 1.2 us)
Sparse Core Ops, SparseCore 0:
  95.0 54.7 all-gather.1
  364.1 82.2 reduce-scatter.2
  455.1 26.5 reduce-scatter.4
  487.6 143.1 all-reduce.2
where the time goes:
time: 641 us; the launch traced here: 639 us
  waiting for transfers between devices  291 us (45%)
  other arithmetic  141 us (22%)
  local copies, waits for them, and re-layouts  137 us (21%)
  matrix products  31 us (5%)
  starting transfers between devices  17.3 us (3%)
  between operations  14.3 us (2%)
  blocking collectives  7.6 us (1%)
    psum x1, waiting for transfers between devices, on_device(): first_total = lax.psum(first_local, ('sample', 'row', 'col'))  141 us
    unnamed x17, other arithmetic  137 us
    reduce_scatter x1, waiting for transfers between devices, on_device(): own_cols = lax.psum_scatter(terms, 'col', scatter_dimension=2, tiled=True)  72.7 us
    slice x9, local copies, waits for them, and re-layouts, taps_of(): padded[:, row_off:row_off + 2 * out_rows:2, col_off:col_off + 2 * out_col...  54.1 us
    all_gather x1, waiting for transfers between devices, on_device(): strip = lax.all_gather(first_act, 'col', axis=2, tiled=True)  52.3 us
    slice x9, local copies, waits for them, and re-layouts, on_device(): strip_ext[:, row_off:row_off + 2 * quarter:2, col_off:col_off + 2 * out_c...  42.9 us
    reduce_scatter x1, waiting for transfers between devices, on_device(): lax.psum_scatter(kernel_local, 'row', scatter_dimension=0, tiled=True)  25 us
    ppermute x4, starting transfers between devices, from_behind(): lax.ppermute(value, axis, [(source, source + steps) for source in range(i...  17.1 us
  transfers between devices with their start and end apart: 8, of which 4 were waited for; matrix products, arithmetic and copies ran while one was open for 7% of the time, Pallas kernels for 0%

commit v1 on v0

v1 whole, which is shorter than its diff:
```python
import jax
import jax.numpy as jnp
from jax import lax
from jax.experimental import pallas as pl
from jax.experimental.pallas import tpu as pltpu
from jax.sharding import PartitionSpec as P

C0 = 64
C1 = 128
BF = jnp.bfloat16
F32 = jnp.float32
MESH = pl.DeviceIdType.MESH


def nn(a, b):
    return lax.dot_general(a, b, (((1,), (0,)), ((), ())), preferred_element_type=F32)


def nt(a, b):
    return lax.dot_general(a, b, (((1,), (1,)), ((), ())), preferred_element_type=F32)


def tn(a, b):
    return lax.dot_general(a, b, (((0,), (0,)), ((), ())), preferred_element_type=F32)


def eye(rows, cols):
    i = lax.broadcasted_iota(jnp.int32, (rows, cols), 0)
    j = lax.broadcasted_iota(jnp.int32, (rows, cols), 1)
    return (i == j).astype(F32).astype(BF)


def at16(index, size):
    return pl.ds(pl.multiple_of(index * size, size), size)


class Exchange:
    def __init__(self, n, me, device, source, target, send, recv):
        self.n, self.me, self.device = n, me, device
        self.source, self.target, self.send, self.recv = source, target, send, recv

    def copy(self, k, slot):
        peer = lax.rem(self.me + k, self.n)
        where = self.me if slot is None else peer
        return pltpu.make_async_remote_copy(
            src_ref=self.source(peer),
            dst_ref=self.target(where),
            send_sem=self.send.at[k],
            recv_sem=self.recv.at[where],
            device_id=self.device(peer),
            device_id_type=MESH,
        )

    def loop(self, act):
        def body(k, carry):
            act(k)
            return carry

        lax.fori_loop(1, self.n, body, 0)

    def start(self):
        self.loop(lambda k: self.copy(k, None).start())

    def wait_recv(self):
        self.loop(lambda k: self.copy(k, "peer").wait_recv())

    def wait_send(self):
        self.loop(lambda k: self.copy(k, None).wait_send())


def kernel(
    img, w1, wd, cot, out1, out2,
    xe, xr, w1f, wf, wdf, wt, cotf, cs, cr, q, acte, acto, sle, slo, patch,
    gwt, ra, gt, ra2, sb, rb, sb2, rb2, gtall, o2,
    local_sem, halo_send, halo_recv, w_send, w_recv, c_send, c_recv, a_send, a_recv,
    a2_send, a2_recv, b_send, b_recv, b2_send, b2_recv, g_send, g_recv,
):
    n_sample, n_row, n_col = (lax.axis_size(name) for name in ("sample", "row", "col"))
    n_group = n_sample * n_row
    s, r, c = (lax.axis_index(name) for name in ("sample", "row", "col"))
    group = s * n_row + r

    def col_device(p):
        return (s, r, p)

    def group_device(p):
        return (p // n_row, lax.rem(p, n_row), c)

    own = pltpu.make_async_copy(
        img.at[0], xe.at[pl.ds(16, 64), pl.ds(256, 4096)], local_sem
    )
    own.start()

    barrier = pltpu.get_barrier_semaphore()

    def greet_col(k, carry):
        pl.semaphore_signal(
            barrier, inc=1, device_id=col_device(lax.rem(c + k, n_col)), device_id_type=MESH
        )
        return carry

    def greet_group(k, carry):
        pl.semaphore_signal(
            barrier, inc=1, device_id=group_device(lax.rem(group + k, n_group)), device_id_type=MESH
        )
        return carry

    lax.fori_loop(1, n_col, greet_col, 0)
    lax.fori_loop(1, n_group, greet_group, 0)
    down, right = lax.rem(r + 1, n_row), lax.rem(c + 1, n_col)
    up, left = lax.rem(r + n_row - 1, n_row), lax.rem(c + n_col - 1, n_col)
    for corner in ((s, down, right), (s, up, left)):
        pl.semaphore_signal(barrier, inc=1, device_id=corner, device_id_type=MESH)

    wdf[...] = jnp.zeros(wdf.shape, F32)
    wdf[:, 0:32] = wd[...].astype(F32)
    unit32 = eye(32, 128)
    for tap in range(9):
        piece = wdf[pl.ds(tap, 128, stride=9), :].astype(BF)
        wt[at16(c, 32), 128 * tap : 128 * tap + 128] = nt(unit32, piece).astype(BF)

    cotf[...] = cot[0].reshape(512, 128).astype(F32)
    unit128 = eye(128, 128)
    for g in range(4):
        rows = [cotf[pl.ds(4 * g + k, 32, stride=16), :] for k in range(4)]
        cs[g] = nt(unit128, jnp.concatenate(rows, 0).astype(BF)).astype(BF)
    cr[c] = cs[:, at16(c, 16), :]

    pl.semaphore_wait(barrier, (n_col - 1) + (n_group - 1) + 2)

    def halo(index, source, target, device):
        return pltpu.make_async_remote_copy(
            src_ref=source,
            dst_ref=target,
            send_sem=halo_send.at[index],
            recv_sem=halo_recv.at[index],
            device_id=device,
            device_id_type=MESH,
        )

    to_down = halo(0, img.at[0, pl.ds(48, 16), :], xe.at[pl.ds(0, 16), pl.ds(256, 4096)], (s, down, c))
    to_right = halo(1, img.at[0, :, pl.ds(3840, 256)], xe.at[pl.ds(16, 64), pl.ds(0, 256)], (s, r, right))
    to_corner = halo(
        2, img.at[0, pl.ds(48, 16), pl.ds(3840, 256)], xe.at[pl.ds(0, 16), pl.ds(0, 256)], (s, down, right)
    )
    sends_down, sends_right = r < n_row - 1, c < n_col - 1
    has_up, has_left = r > 0, c > 0

    @pl.when(sends_down)
    def _():
        to_down.start()

    @pl.when(sends_right)
    def _():
        to_right.start()

    @pl.when(jnp.logical_and(sends_down, sends_right))
    def _():
        to_corner.start()

    weights = Exchange(
        n_col, c, col_device, lambda p: wt.at[at16(c, 32), :], lambda p: wt.at[at16(p, 32), :], w_send, w_recv
    )
    cotangents = Exchange(
        n_col, c, col_device, lambda p: cs.at[:, at16(p, 16), :], lambda p: cr.at[p], c_send, c_recv
    )
    weights.start()
    cotangents.start()

    @pl.when(jnp.logical_not(has_up))
    def _():
        xe[0:16, 256:4352] = jnp.zeros((16, 4096), BF)

    @pl.when(jnp.logical_not(has_left))
    def _():
        xe[16:80, 0:256] = jnp.zeros((64, 256), BF)

    @pl.when(jnp.logical_not(jnp.logical_and(has_up, has_left)))
    def _():
        xe[0:16, 0:256] = jnp.zeros((16, 256), BF)

    w1f[...] = w1[...].astype(F32)
    for ta in range(3):
        wf[ta, 0:64] = jnp.zeros((64, 128), BF)
        for tb in range(3):
            wf[ta, 64 * tb + 64 : 64 * tb + 128] = w1f[pl.ds(3 * ta + tb, 64, stride=9), :].astype(BF)

    own.wait()

    @pl.when(has_up)
    def _():
        to_down.wait_recv()

    @pl.when(has_left)
    def _():
        to_right.wait_recv()

    @pl.when(jnp.logical_and(has_up, has_left))
    def _():
        to_corner.wait_recv()

    row = lax.broadcasted_iota(jnp.int32, (112, 80), 0)
    col = lax.broadcasted_iota(jnp.int32, (112, 80), 1)
    pick = (col == 13 + 4 * (row % 16) + row // 16).astype(F32).astype(BF)
    for t in range(17):
        got = nn(pick, xe[:, 256 * t : 256 * t + 256]).astype(BF)
        xr[:, t] = got.reshape(7, 16, 256)

    def even_of(p):
        return xr[p].reshape(272, 256)

    def odd_of(p):
        return jnp.concatenate([xr[p, 0:16, :, 128:256], xr[p, 1:17, :, 0:128]], 2).reshape(256, 256)

    for a in range(3):
        even = nn(even_of(2 * a), wf[0]) + nn(even_of(2 * a + 1), wf[1]) + nn(even_of(2 * a + 2), wf[2])
        odd = nn(odd_of(2 * a), wf[0]) + nn(odd_of(2 * a + 1), wf[1]) + nn(odd_of(2 * a + 2), wf[2])
        for pre, act, slope, count in ((even, acte, sle, 17), (odd, acto, slo, 16)):
            sig = jax.nn.sigmoid(pre)
            act[a] = (pre * sig).astype(BF).reshape(count, 16, 128)
            slope[a] = (sig * (1.0 + pre * (1.0 - sig))).reshape(count, 16, 128)

    for a in range(3):
        patch[:, 384 * a : 384 * a + 128] = acte[a, 0:16].reshape(256, 128)
        patch[:, 384 * a + 128 : 384 * a + 256] = acto[a].reshape(256, 128)
        patch[:, 384 * a + 256 : 384 * a + 384] = acte[a, 1:17].reshape(256, 128)

    weights.wait_recv()
    pre = nt(patch[...], wt[...])

    cotangents.wait_recv()
    lane = lax.broadcasted_iota(jnp.int32, (16, 128), 1) // 32
    for g in range(4):
        for half in range(2):
            tiles = [cr[4 * half + i, g].astype(F32) for i in range(4)]
            for k in range(4):
                mixed = jnp.zeros((16, 128), F32)
                for i in range(4):
                    shift = (32 * (i - k)) % 128
                    moved = pltpu.roll(tiles[i], shift, 1) if shift else tiles[i]
                    mixed = jnp.where(lane == i, moved, mixed)
                q[half, 16 * (4 * g + k) : 16 * (4 * g + k) + 16] = mixed
    cotangent = jnp.concatenate(
        [
            jnp.concatenate([q[half, pl.ds(n, 16, stride=16), :] for half in range(2)], 1)
            for n in range(16)
        ],
        0,
    )

    sig = jax.nn.sigmoid(pre)
    dg = (cotangent * (sig * (1.0 + pre * (1.0 - sig)))).astype(BF)

    gwt[...] = tn(dg, patch[...]).astype(BF)
    deep_a = Exchange(
        n_col, c, col_device, lambda p: gwt.at[at16(p, 32), :], lambda p: ra.at[p], a_send, a_recv
    )
    deep_a.start()
    ra[c] = gwt[at16(c, 32), :]

    back = nn(dg, wt[...])
    empty = jnp.zeros((1, 16, 128), F32)
    totals = [jnp.zeros((128, 256), F32) for _ in range(3)]
    for a in range(3):
        part = [back[:, 384 * a + 128 * b : 384 * a + 128 * b + 128].reshape(16, 16, 128) for b in range(3)]
        even = jnp.concatenate([part[0], empty], 0) + jnp.concatenate([empty, part[2]], 0)
        even = (even * sle[a]).reshape(272, 128).astype(BF)
        odd = (part[1] * slo[a]).reshape(256, 128).astype(BF)
        for ta in range(3):
            totals[ta] += tn(even, even_of(2 * a + ta)) + tn(odd, odd_of(2 * a + ta))
    for ta in range(3):
        gt[:, 256 * ta : 256 * ta + 256] = totals[ta].astype(BF)
    first_a = Exchange(
        n_col, c, col_device, lambda p: gt.at[at16(p, 16), :], lambda p: ra2.at[p], a2_send, a2_recv
    )
    first_a.start()
    ra2[c] = gt[at16(c, 16), :]

    deep_a.wait_recv()
    total = ra[0].astype(F32)
    for p in range(1, n_col):
        total = total + ra[p].astype(F32)
    for g in range(3):
        taps = range(4 * g, min(4 * g + 4, 9))
        block = [total[:, 128 * tap : 128 * tap + 128] for tap in taps]
        if len(block) < 4:
            block.append(jnp.zeros((128 - 32 * len(block), 128), F32))
        sb[g] = nt(unit128, jnp.concatenate(block, 0).astype(BF)).astype(BF)
    deep_b = Exchange(
        n_group, group, group_device,
        lambda p: sb.at[:, at16(lax.rem(p, n_row), 16), :], lambda p: rb.at[p], b_send, b_recv,
    )
    deep_b.start()
    rb[group] = sb[:, at16(r, 16), :]

    first_a.wait_recv()
    total = ra2[0].astype(F32)
    for p in range(1, n_col):
        total = total + ra2[p].astype(F32)
    sb2[...] = total.astype(BF)
    first_b = Exchange(n_group, group, group_device, lambda p: sb2, lambda p: rb2.at[p], b2_send, b2_recv)
    first_b.start()
    rb2[group] = sb2[...]

    deep_b.wait_recv()
    total = rb[0].astype(F32)
    for p in range(1, n_group):
        total = total + rb[p].astype(F32)
    for tap in range(9):
        block = total[tap // 4]
        if tap % 4:
            block = pltpu.roll(block, 128 - 32 * (tap % 4), 1)
        o2[pl.ds(tap, 16, stride=9), :] = block
    out2[...] = o2[:, 0:32]

    first_b.wait_recv()
    total = rb2[0].astype(F32)
    for p in range(1, n_group):
        total = total + rb2[p].astype(F32)
    gtall[at16(c, 16), :] = total.astype(BF)
    first_g = Exchange(
        n_col, c, col_device,
        lambda p: gtall.at[at16(c, 16), :], lambda p: gtall.at[at16(p, 16), :], g_send, g_recv,
    )
    first_g.start()
    first_g.wait_recv()
    unit256 = eye(256, 256)
    for ta in range(3):
        block = nt(unit256, gtall[:, 256 * ta : 256 * ta + 256])
        for tb in range(3):
            out1[pl.ds(3 * ta + tb, 64, stride=9), :] = block[64 * tb + 64 : 64 * tb + 128]

    @pl.when(sends_down)
    def _():
        to_down.wait_send()

    @pl.when(sends_right)
    def _():
        to_right.wait_send()

    @pl.when(jnp.logical_and(sends_down, sends_right))
    def _():
        to_corner.wait_send()

    for exchange in (weights, cotangents, deep_a, first_a, deep_b, first_b, first_g):
        exchange.wait_send()


def on_device(images, first_weight, deep_weight, deep_cotangent):
    n_col = lax.axis_size("col")
    n_group = lax.axis_size("row") * lax.axis_size("sample")
    vmem = pl.BlockSpec(memory_space=pltpu.VMEM)
    dma = pltpu.SemaphoreType.DMA
    return pl.pallas_call(
        kernel,
        out_shape=(
            jax.ShapeDtypeStruct((576, 128), F32),
            jax.ShapeDtypeStruct((144, 32), F32),
        ),
        in_specs=[pl.BlockSpec(memory_space=pl.ANY), vmem, vmem, vmem],
        out_specs=(vmem, vmem),
        scratch_shapes=[
            pltpu.VMEM((80, 4352), BF),
            pltpu.VMEM((7, 17, 16, 256), BF),
            pltpu.VMEM((576, 128), F32),
            pltpu.VMEM((3, 256, 128), BF),
            pltpu.VMEM((1152, 128), F32),
            pltpu.VMEM((256, 1152), BF),
            pltpu.VMEM((512, 128), F32),
            pltpu.VMEM((4, 128, 128), BF),
            pltpu.VMEM((n_col, 4, 16, 128), BF),
            pltpu.VMEM((2, 256, 128), F32),
            pltpu.VMEM((3, 17, 16, 128), BF),
            pltpu.VMEM((3, 16, 16, 128), BF),
            pltpu.VMEM((3, 17, 16, 128), F32),
            pltpu.VMEM((3, 16, 16, 128), F32),
            pltpu.VMEM((256, 1152), BF),
            pltpu.VMEM((256, 1152), BF),
            pltpu.VMEM((n_col, 32, 1152), BF),
            pltpu.VMEM((128, 768), BF),
            pltpu.VMEM((n_col, 16, 768), BF),
            pltpu.VMEM((3, 128, 128), BF),
            pltpu.VMEM((n_group, 3, 16, 128), BF),
            pltpu.VMEM((16, 768), BF),
            pltpu.VMEM((n_group, 16, 768), BF),
            pltpu.VMEM((128, 768), BF),
            pltpu.VMEM((144, 128), F32),
            dma,
            dma((3,)), dma((3,)),
            dma((n_col,)), dma((n_col,)),
            dma((n_col,)), dma((n_col,)),
            dma((n_col,)), dma((n_col,)),
            dma((n_col,)), dma((n_col,)),
            dma((n_group,)), dma((n_group,)),
            dma((n_group,)), dma((n_group,)),
            dma((n_col,)), dma((n_col,)),
        ],
        compiler_params=pltpu.CompilerParams(
            collective_id=0, has_side_effects=True, vmem_limit_bytes=40 * 2**20
        ),
    )(images, first_weight, deep_weight, deep_cotangent)


def solution(mesh):
    return jax.shard_map(
        on_device,
        mesh=mesh,
        in_specs=(P("sample", "row", "col"), P(), P(None, "col"), P("sample", "col", "row", None)),
        out_specs=(P(), P("row", "col")),
        check_vma=False,
    )
```

time: 641 us -> 51.2 us (0.08)
  waiting for transfers between devices: 291 us -> 0 us
  other arithmetic: 141 us -> 0 us
  local copies, waits for them, and re-layouts: 137 us -> 3.59 us
  Pallas kernels: 0 us -> 46.7 us
  matrix products: 31 us -> 0 us
  starting transfers between devices: 17.3 us -> 0 us
  between operations: 14.3 us -> 0.68 us
  blocking collectives: 7.6 us -> 0 us
    psum x1 -> x0, waiting for transfers between devices: 141 us -> none  [on_device(): first_total = lax.psum(first_local, ('sample', 'row', 'col'))]
    unnamed x17 -> x0, other arithmetic: 137 us -> none
    slice x35 -> x0, local copies, waits for them, and re-layouts: 105 us -> none  [the longest x9 54.1 us: taps_of(): padded[:, row_off:row_off + 2 * out_rows:2, col_off:col_off + 2 * out_col...]
    reduce_scatter x2 -> x0, waiting for transfers between devices: 97.7 us -> none  [the longest x1 72.7 us: on_device(): own_cols = lax.psum_scatter(terms, 'col', scatter_dimension=2, tiled=True)]
    all_gather x1 -> x0, waiting for transfers between devices: 52.3 us -> none  [on_device(): strip = lax.all_gather(first_act, 'col', axis=2, tiled=True)]
    pallas_call x0 -> x1, Pallas kernels: none -> 46.7 us  [on_device(): pl.pallas_call(kernel, out_shape=(jax.ShapeDtypeStruct((576, 128), F32),...]
    dot_general x29 -> x0, matrix products: 31 us -> none  [the longest x9 11.9 us: on_device(): jnp.dot(kernel_taps[:, 3 * row_off + col_off, :], deep_grad, preferred_el...]
    ppermute x4 -> x0, starting transfers between devices: 17.1 us -> none  [from_behind(): lax.ppermute(value, axis, [(source, source + steps) for source in range(i...]
  transfers between devices with their start and end apart: 8 -> 0, of which waited for: 4 -> 0; matrix products, arithmetic and copies ran while one was open for 7% -> 0% of each run, Pallas kernels for 0% -> 0%
where the time goes in v1:
time: 51.2 us; the launch traced here: 50.9 us
  Pallas kernels  46.7 us (91%)
  local copies, waits for them, and re-layouts  3.59 us (7%)
  between operations  0.68 us (1%)
    pallas_call x1, Pallas kernels, on_device(): pl.pallas_call(kernel, out_shape=(jax.ShapeDtypeStruct((576, 128), F32),...  46.7 us
    unnamed x8, local copies, waits for them, and re-layouts  2.9 us

profile of v1, /device:TPU:1, one launch (start us, length us, event | category | flops | bytes accessed | tf_op | source)
XLA Modules:
  0.0 50.9 jit_solution(16514634926000700955)
XLA Ops:
  0.6 0.0 copy-start.2
  0.6 0.0 copy-start.1
  0.7 1.1 %copy.6.wd = bf16[1152,32]{1,0:T(8,128)(2,1)S(1)} copy(bf16[1152,32]{0,1:T(8,128)(2,1)} %param.6) | data formatting | bytes 147456 | tf_op args[2]
  1.8 0.0 copy-done.2
  1.8 0.0 copy-done.1
  1.8 0.0 copy-start
  1.8 1.0 %copy-done = bf16[1,64,4096]{2,1,0:T(8,128)(2,1)S(1)} copy-done((bf16[1,64,4096]{2,1,0:T(8,128)(2,1)S(1)}, bf16[1,64,4096]{2,1,0:T(8,128)(2,1)}, u32[]{:S(2)}) %copy-start) | copy-done | bytes 524312
  2.9 46.7 %shard_map.59 = (f32[576,128]{1,0:T(8,128)S(1)}, f32[144,32]{1,0:T(8,128)S(1)}) custom-call(bf16[1,64,4096]{2,1,0:T(8,128)(2,1)S(1)} %copy-done, bf16[576,128]{1,0:T(8,128)(2,1)S(1)} %copy-done.1, bf16[1152,32]{1,0:T(8,128)(2,1)S(1)} %copy.6.wd, bf16[1,32,16,128]{3,2,1,0:T(8,128)(2,1)S(1)} %copy-done.2), custom_call_target="tpu_custom_call" | custom-call | tf_op jit(solution)/shard_map/pallas_call | solution.py:354
  49.5 0.7 %copy.7 = f32[144,32]{0,1:T(8,128)} copy(f32[144,32]{1,0:T(8,128)S(1)} %get-tuple-element.3) | data formatting | bytes 36864 | tf_op jit(solution)/shard_map/pallas_call | solution.py:354
  50.2 0.7 %copy.9 = f32[576,128]{1,0:T(8,128)} copy(f32[576,128]{1,0:T(8,128)S(1)} %get-tuple-element.6) | data formatting | bytes 589824
Async XLA Ops:
  0.6 1.2 %copy-start.2 = (bf16[1,32,16,128]{3,2,1,0:T(8,128)(2,1)S(1)}, bf16[1,32,16,128]{3,2,1,0:T(8,128)(2,1)}, u32[]{:S(2)}) copy-start(bf16[1,32,16,128]{3,2,1,0:T(8,128)(2,1)} %cot.1) | copy-start | bytes 393220
  0.6 1.2 %copy-start.1 = (bf16[576,128]{1,0:T(8,128)(2,1)S(1)}, bf16[576,128]{1,0:T(8,128)(2,1)}, u32[]{:S(2)}) copy-start(bf16[576,128]{1,0:T(8,128)(2,1)} %w1.1) | copy-start | bytes 442372
  1.8 1.0 %copy-start = (bf16[1,64,4096]{2,1,0:T(8,128)(2,1)S(1)}, bf16[1,64,4096]{2,1,0:T(8,128)(2,1)}, u32[]{:S(2)}) copy-start(bf16[1,64,4096]{2,1,0:T(8,128)(2,1)} %img.1) | copy-start | bytes 1572868

commit v2 on v1

v2 whole, which is shorter than its diff:
```python
import jax
import jax.numpy as jnp
from jax import lax
from jax.experimental import pallas as pl
from jax.experimental.pallas import tpu as pltpu
from jax.sharding import PartitionSpec as P

BF = jnp.bfloat16
F32 = jnp.float32
MESH = pl.DeviceIdType.MESH

N_ROW = 8
N_COL = 8
N_BOTH = 16


def nn(a, b):
    return lax.dot_general(a, b, (((1,), (0,)), ((), ())), preferred_element_type=F32)


def nt(a, b):
    return lax.dot_general(a, b, (((1,), (1,)), ((), ())), preferred_element_type=F32)


def tn(a, b):
    return lax.dot_general(a, b, (((0,), (0,)), ((), ())), preferred_element_type=F32)


def eye(size):
    i = lax.broadcasted_iota(jnp.int32, (size, size), 0)
    j = lax.broadcasted_iota(jnp.int32, (size, size), 1)
    return (i == j).astype(F32).astype(BF)


def rows_of(index, size):
    return pl.ds(pl.multiple_of(index * size, size), size)


def remote(src, dst, send, recv, device):
    return pltpu.make_async_remote_copy(
        src_ref=src, dst_ref=dst, send_sem=send, recv_sem=recv, device_id=device, device_id_type=MESH
    )


class Fan:
    def __init__(self, pairs):
        self.pairs = list(pairs)

    def start(self):
        for out, _ in self.pairs:
            out.start()

    def wait_recv(self):
        for _, arriving in self.pairs:
            arriving.wait_recv()

    def wait_send(self):
        for out, _ in self.pairs:
            out.wait_send()


def kernel(
    img, w1, wd, cot, out1, out2,
    xe, w1v, wdv, cotv, xr, w1f, wf, wdf, wt, cotf, cs, cr, q, acte, acto, sle, slo, patch,
    gwt, pair_in, half, ra, gt, fa, sb, rb, sb2, rb2, gtall, o2,
    in_sem, halo_s, halo_r, w_s, w_r, v_s, v_r, c_s, c_r, d0_s, d0_r, d1_s, d1_r, d2_s, d2_r,
    f1_s, f1_r, f2_s, f2_r, f3_s, f3_r,
):
    s, r, c = (lax.axis_index(name) for name in ("sample", "row", "col"))
    core = lax.rem(r, 2)
    partner = r + 1 - 2 * core
    group = s * N_ROW + r
    plane = s * N_COL + c

    inputs = [
        pltpu.make_async_copy(cot.at[0], cotv, in_sem.at[0]),
        pltpu.make_async_copy(wd, wdv, in_sem.at[1]),
        pltpu.make_async_copy(w1, w1v, in_sem.at[2]),
        pltpu.make_async_copy(img.at[0], xe.at[pl.ds(16, 64), pl.ds(256, 4096)], in_sem.at[3]),
    ]

    def in_plane(k, sign=1):
        return (lax.rem(s + k // N_COL, 2), lax.rem(c + N_COL + sign * (k % N_COL), N_COL))

    def in_group(k, sign=1):
        return (lax.rem(s + k // N_ROW, 2), lax.rem(r + N_ROW + sign * (k % N_ROW), N_ROW))

    down, right = lax.rem(r + 1, N_ROW), lax.rem(c + 1, N_COL)
    up, left = lax.rem(r + N_ROW - 1, N_ROW), lax.rem(c + N_COL - 1, N_COL)

    barrier = pltpu.get_barrier_semaphore()
    greeted = [(s, down, right), (s, up, left)]
    for k in range(1, N_BOTH):
        ps, pc = in_plane(k)
        greeted.append((ps, r, pc))
    for k in range(1, N_BOTH):
        if k != N_ROW:
            ps, pr = in_group(k)
            greeted.append((ps, pr, c))
    for device in greeted:
        pl.semaphore_signal(barrier, inc=1, device_id=device, device_id_type=MESH)
    for copy in inputs:
        copy.start()

    unit = eye(128)

    inputs[0].wait()
    cotf[...] = cotv[...].reshape(512, 128).astype(F32)
    for g in range(4):
        picked = [cotf[pl.ds(4 * g + k, 32, stride=16), :] for k in range(4)]
        cs[g] = nt(unit, jnp.concatenate(picked, 0).astype(BF)).astype(BF)
    cr[0] = cs[:, rows_of(c, 16), :]

    inputs[1].wait()
    blank = jnp.zeros((96, 128), BF)
    for j in range(9):
        wdf[128 * j : 128 * j + 128] = nt(unit, jnp.concatenate([wdv[:, 128 * j : 128 * j + 128], blank], 0))
    for tap in range(9):
        piece = wdf[pl.ds(tap, 128, stride=9), :].astype(BF)
        wt[rows_of(c, 32), 128 * tap : 128 * tap + 128] = nt(unit, piece)[0:32].astype(BF)

    inputs[2].wait()
    w1f[...] = w1v[...].astype(F32)
    for ta in range(3):
        wf[ta, 0:64] = jnp.zeros((64, 128), BF)
        for tb in range(3):
            wf[ta, 64 * tb + 64 : 64 * tb + 128] = w1f[pl.ds(3 * ta + tb, 64, stride=9), :].astype(BF)

    pl.semaphore_wait(barrier, len(greeted))

    def halo(index, source, target, device):
        return remote(source, target, halo_s.at[index], halo_r.at[index], device)

    to_down = halo(0, img.at[0, pl.ds(48, 16), :], xe.at[pl.ds(0, 16), pl.ds(256, 4096)], (s, down, c))
    to_right = halo(1, img.at[0, :, pl.ds(3840, 256)], xe.at[pl.ds(16, 64), pl.ds(0, 256)], (s, r, right))
    to_corner = halo(
        2, img.at[0, pl.ds(48, 16), pl.ds(3840, 256)], xe.at[pl.ds(0, 16), pl.ds(0, 256)], (s, down, right)
    )
    sends_down, sends_right = r < N_ROW - 1, c < N_COL - 1
    has_up, has_left = r > 0, c > 0

    @pl.when(jnp.logical_and(sends_down, sends_right))
    def _():
        to_corner.start()

    @pl.when(sends_right)
    def _():
        to_right.start()

    z, xhi = c // 2, lax.rem(c, 2)

    def across(dz, dx, sign=1):
        return lax.rem(s + dx, 2), lax.rem(z + 4 + sign * dz, 4) * 2 + lax.rem(xhi + dx, 2)

    def half_shard(col, which):
        return wt.at[pl.ds(pl.multiple_of(32 * col + 16 * which, 16), 16), :]

    far_first = ((2, 1), (1, 1), (3, 1), (2, 0), (1, 0), (3, 0), (0, 1))
    weights, handed_on = [], []
    for k, (dz, dx) in enumerate(far_first):
        ps, pc = across(dz, dx)
        qs, qc = across(dz, dx, -1)
        weights.append(
            (
                remote(half_shard(c, core), half_shard(c, core), w_s.at[k], w_r.at[k], (ps, r, pc)),
                remote(half_shard(qc, core), half_shard(qc, core), w_s.at[k], w_r.at[k], (qs, r, qc)),
            )
        )
        handed_on.append(
            (
                remote(half_shard(qc, core), half_shard(qc, core), v_s.at[k], v_r.at[k], (s, partner, c)),
                remote(half_shard(qc, 1 - core), half_shard(qc, 1 - core), v_s.at[k], v_r.at[k], (s, partner, c)),
            )
        )
    weights, handed_on = Fan(weights), Fan(handed_on)
    weights.start()

    @pl.when(sends_down)
    def _():
        to_down.start()

    cotangents = []
    for k, (dz, dx) in enumerate(far_first):
        _, pc = across(dz, dx)
        _, qc = across(dz, dx, -1)
        cotangents.append(
            (
                remote(cs.at[:, rows_of(pc, 16), :], cr.at[dz + 4 * dx], c_s.at[k], c_r.at[k], (s, r, pc)),
                remote(cs.at[:, rows_of(qc, 16), :], cr.at[dz + 4 * dx], c_s.at[k], c_r.at[k], (s, r, qc)),
            )
        )
    cotangents = Fan(cotangents)
    cotangents.start()

    @pl.when(jnp.logical_not(has_up))
    def _():
        xe[0:16, 256:4352] = jnp.zeros((16, 4096), BF)

    @pl.when(jnp.logical_not(has_left))
    def _():
        xe[16:80, 0:256] = jnp.zeros((64, 256), BF)

    @pl.when(jnp.logical_not(jnp.logical_and(has_up, has_left)))
    def _():
        xe[0:16, 0:256] = jnp.zeros((16, 256), BF)

    inputs[3].wait()

    @pl.when(has_up)
    def _():
        to_down.wait_recv()

    @pl.when(has_left)
    def _():
        to_right.wait_recv()

    @pl.when(jnp.logical_and(has_up, has_left))
    def _():
        to_corner.wait_recv()

    row = lax.broadcasted_iota(jnp.int32, (112, 80), 0)
    col = lax.broadcasted_iota(jnp.int32, (112, 80), 1)
    pick = (col == 13 + 4 * (row % 16) + row // 16).astype(F32).astype(BF)
    for t in range(17):
        got = nn(pick, xe[:, 256 * t : 256 * t + 256]).astype(BF)
        xr[:, t] = got.reshape(7, 16, 256)

    def even_of(p):
        return xr[p].reshape(272, 256)

    def odd_of(p):
        return jnp.concatenate([xr[p, 0:16, :, 128:256], xr[p, 1:17, :, 0:128]], 2).reshape(256, 256)

    for a in range(3):
        even = nn(even_of(2 * a), wf[0]) + nn(even_of(2 * a + 1), wf[1]) + nn(even_of(2 * a + 2), wf[2])
        odd = nn(odd_of(2 * a), wf[0]) + nn(odd_of(2 * a + 1), wf[1]) + nn(odd_of(2 * a + 2), wf[2])
        for pre, act, slope, count in ((even, acte, sle, 17), (odd, acto, slo, 16)):
            sig = jax.nn.sigmoid(pre)
            act[a] = (pre * sig).astype(BF).reshape(count, 16, 128)
            slope[a] = (sig * (1.0 + pre * (1.0 - sig))).reshape(count, 16, 128)

    for a in range(3):
        patch[:, 384 * a : 384 * a + 128] = acte[a, 0:16].reshape(256, 128)
        patch[:, 384 * a + 128 : 384 * a + 256] = acto[a].reshape(256, 128)
        patch[:, 384 * a + 256 : 384 * a + 384] = acte[a, 1:17].reshape(256, 128)

    for k in range(6, -1, -1):
        weights.pairs[k][1].wait_recv()
        handed_on.pairs[k][0].start()

    cotangents.wait_recv()
    lane = lax.broadcasted_iota(jnp.int32, (16, 128), 1)
    quarter = lane // 32
    def from_col(col):
        return lax.rem(z + 4 - col // 2, 4) + 4 * lax.rem(xhi + col % 2, 2)

    for half_of in range(2):
        slots = [from_col(4 * half_of + i) for i in range(4)]
        for g in range(4):
            tiles = [cr[slots[i], g].astype(F32) for i in range(4)]
            for k in range(4):
                mixed = jnp.zeros((16, 128), F32)
                for i in range(4):
                    shift = (32 * (i - k)) % 128
                    moved = pltpu.roll(tiles[i], shift, 1) if shift else tiles[i]
                    mixed = jnp.where(quarter == i, moved, mixed)
                q[half_of, 16 * (4 * g + k) : 16 * (4 * g + k) + 16] = mixed
    cotangent = jnp.concatenate(
        [jnp.concatenate([q[h, pl.ds(n, 16, stride=16), :] for h in range(2)], 1) for n in range(16)], 0
    )

    handed_on.wait_recv()
    pre = nt(patch[...], wt[...])
    sig = jax.nn.sigmoid(pre)
    dg = (cotangent * (sig * (1.0 + pre * (1.0 - sig)))).astype(BF)

    back = nn(dg, wt[...])
    empty = jnp.zeros((1, 16, 128), F32)
    totals = [jnp.zeros((128, 256), F32) for _ in range(3)]
    for a in range(3):
        part = [back[:, 384 * a + 128 * b : 384 * a + 128 * b + 128].reshape(16, 16, 128) for b in range(3)]
        even = jnp.concatenate([part[0], empty], 0) + jnp.concatenate([empty, part[2]], 0)
        odd = part[1]
        if a == 1:
            even, odd = even.astype(BF).astype(F32), odd.astype(BF).astype(F32)
        even = (even * sle[a]).reshape(272, 128).astype(BF)
        odd = (odd * slo[a]).reshape(256, 128).astype(BF)
        for ta in range(3):
            totals[ta] += tn(even, even_of(2 * a + ta)) + tn(odd, odd_of(2 * a + ta))
    for ta in range(3):
        gt[:, 128 * ta : 128 * ta + 128] = totals[ta][:, 128:256].astype(BF)
    low = lax.broadcasted_iota(jnp.int32, (128, 128), 1) < 64
    both = jnp.where(low, pltpu.roll(totals[1][:, 0:128], 64, 1), totals[0][:, 0:128])
    gt[:, 384:512] = both.astype(BF)
    gt[:, 512:640] = totals[2][:, 0:128].astype(BF)

    first1 = []
    for k in range(1, N_ROW):
        pr, qr = lax.rem(r + k, N_ROW), lax.rem(r + N_ROW - k, N_ROW)
        first1.append(
            (
                remote(gt.at[rows_of(pr, 16), :], fa.at[k], f1_s.at[k], f1_r.at[k], (s, pr, c)),
                remote(gt.at[rows_of(qr, 16), :], fa.at[k], f1_s.at[k], f1_r.at[k], (s, qr, c)),
            )
        )
    first1 = Fan(first1)
    first1.start()

    gwt[...] = tn(dg, patch[...]).astype(BF).reshape(8, 2, 16, 1152)
    pair = remote(gwt.at[:, 1 - core], pair_in, d0_s.at[0], d0_r.at[0], (s, partner, c))
    pair.start()
    pair.wait_recv()
    half[...] = (gwt[:, core].astype(F32) + pair_in[...].astype(F32)).astype(BF)

    deep1 = []
    for k, (dz, dx) in enumerate(far_first):
        ps, pc = across(dz, dx)
        qs, qc = across(dz, dx, -1)
        deep1.append(
            (
                remote(half.at[pc], ra.at[k], d1_s.at[k], d1_r.at[k], (ps, r, pc)),
                remote(half.at[qc], ra.at[k], d1_s.at[k], d1_r.at[k], (qs, r, qc)),
            )
        )
    deep1 = Fan(deep1)
    deep1.start()

    first1.wait_recv()
    total = gt[rows_of(r, 16), :].astype(F32)
    for k in range(1, N_ROW):
        total = total + fa[k].astype(F32)
    sb2[...] = total.astype(BF)
    first2 = []
    for k in range(N_BOTH - 1, 0, -1):
        ps, pc = in_plane(k)
        qs, qc = in_plane(k, -1)
        first2.append(
            (
                remote(sb2, rb2.at[plane], f2_s.at[k], f2_r.at[k], (ps, r, pc)),
                remote(sb2, rb2.at[qs * N_COL + qc], f2_s.at[k], f2_r.at[k], (qs, r, qc)),
            )
        )
    first2 = Fan(first2)
    first2.start()
    rb2[plane] = sb2[...]

    deep1.wait_recv()
    total = half[c].astype(F32)
    for k in range(7):
        total = total + ra[k].astype(F32)
    block = jnp.concatenate([total[:, 128 * tap : 128 * tap + 128] for tap in range(8)], 0)
    sb[0] = nt(unit, block.astype(BF)).astype(BF)
    block = jnp.concatenate([total[:, 1024:1152], jnp.zeros((112, 128), F32)], 0)
    sb[1] = nt(unit, block.astype(BF)).astype(BF)
    deep2 = []
    for k in range(N_BOTH - 1, 0, -1):
        ps, pr = in_group(k)
        qs, qr = in_group(k, -1)
        deep2.append(
            (
                remote(sb.at[:, rows_of(pr, 16), :], rb.at[group], d2_s.at[k], d2_r.at[k], (ps, pr, c)),
                remote(
                    sb.at[:, rows_of(qr, 16), :], rb.at[qs * N_ROW + qr], d2_s.at[k], d2_r.at[k], (qs, qr, c)
                ),
            )
        )
    deep2 = Fan(deep2)
    deep2.start()
    rb[group] = sb[:, rows_of(r, 16), :]

    first2.wait_recv()
    total = rb2[0].astype(F32)
    for p in range(1, N_BOTH):
        total = total + rb2[p].astype(F32)
    gtall[rows_of(r, 16), :] = total.astype(BF)
    first3 = []
    for k in range(1, N_ROW):
        pr, qr = lax.rem(r + k, N_ROW), lax.rem(r + N_ROW - k, N_ROW)
        first3.append(
            (
                remote(gtall.at[rows_of(r, 16), :], gtall.at[rows_of(r, 16), :], f3_s.at[k], f3_r.at[k], (s, pr, c)),
                remote(gtall.at[rows_of(qr, 16), :], gtall.at[rows_of(qr, 16), :], f3_s.at[k], f3_r.at[k], (s, qr, c)),
            )
        )
    first3 = Fan(first3)
    first3.start()

    deep2.wait_recv()
    halves = []
    for which in range(2):
        total = rb[which].astype(F32)
        for p in range(which + 2, N_BOTH, 2):
            total = total + rb[p].astype(F32)
        halves.append(total)
    for tap in range(9):
        lower, upper = (h[tap // 8] for h in halves)
        shift = (128 - 16 * (tap % 8)) % 128
        lower = pltpu.roll(lower, shift, 1) if shift else lower
        upper = pltpu.roll(upper, (shift + 16) % 128, 1) if (shift + 16) % 128 else upper
        o2[pl.ds(tap, 16, stride=9), :] = jnp.where(lane < 16, lower, upper)
    out2[...] = o2[...].T[0:32, 0:144]

    first3.wait_recv()
    places = ((0, 1), (0, 2), (1, 1), (1, 2), (2, 1), (2, 2), (1, 0), (0, 0), None, (2, 0))
    for j in range(5):
        block = nt(unit, gtall[:, 128 * j : 128 * j + 128])
        for i in range(2):
            place = places[2 * j + i]
            if place is not None:
                out1[pl.ds(3 * place[0] + place[1], 64, stride=9), :] = block[64 * i : 64 * i + 64]

    @pl.when(sends_down)
    def _():
        to_down.wait_send()

    @pl.when(sends_right)
    def _():
        to_right.wait_send()

    @pl.when(jnp.logical_and(sends_down, sends_right))
    def _():
        to_corner.wait_send()

    pair.wait_send()
    for fan in (weights, handed_on, cotangents, first1, deep1, first2, deep2, first3):
        fan.wait_send()


def on_device(images, first_weight, deep_weight, deep_cotangent):
    anywhere = pl.BlockSpec(memory_space=pl.ANY)
    vmem = pl.BlockSpec(memory_space=pltpu.VMEM)

    def dma(count):
        return [pltpu.SemaphoreType.DMA((count,))] * 2

    first, deep = pl.pallas_call(
        kernel,
        out_shape=(jax.ShapeDtypeStruct((576, 128), F32), jax.ShapeDtypeStruct((32, 144), F32)),
        in_specs=[anywhere] * 4,
        out_specs=(vmem, vmem),
        scratch_shapes=[
            pltpu.VMEM((80, 4352), BF),
            pltpu.VMEM((576, 128), BF),
            pltpu.VMEM((32, 1152), BF),
            pltpu.VMEM((32, 16, 128), BF),
            pltpu.VMEM((7, 17, 16, 256), BF),
            pltpu.VMEM((576, 128), F32),
            pltpu.VMEM((3, 256, 128), BF),
            pltpu.VMEM((1152, 128), F32),
            pltpu.VMEM((256, 1152), BF),
            pltpu.VMEM((512, 128), F32),
            pltpu.VMEM((4, 128, 128), BF),
            pltpu.VMEM((8, 4, 16, 128), BF),
            pltpu.VMEM((2, 256, 128), F32),
            pltpu.VMEM((3, 17, 16, 128), BF),
            pltpu.VMEM((3, 16, 16, 128), BF),
            pltpu.VMEM((3, 17, 16, 128), F32),
            pltpu.VMEM((3, 16, 16, 128), F32),
            pltpu.VMEM((256, 1152), BF),
            pltpu.VMEM((8, 2, 16, 1152), BF),
            pltpu.VMEM((8, 16, 1152), BF),
            pltpu.VMEM((8, 16, 1152), BF),
            pltpu.VMEM((7, 16, 1152), BF),
            pltpu.VMEM((128, 640), BF),
            pltpu.VMEM((8, 16, 640), BF),
            pltpu.VMEM((2, 128, 128), BF),
            pltpu.VMEM((16, 2, 16, 128), BF),
            pltpu.VMEM((16, 640), BF),
            pltpu.VMEM((16, 16, 640), BF),
            pltpu.VMEM((128, 640), BF),
            pltpu.VMEM((256, 128), F32),
            pltpu.SemaphoreType.DMA((4,)),
            *dma(3), *dma(7), *dma(7), *dma(7), *dma(1), *dma(7), *dma(16), *dma(8), *dma(16), *dma(8),
        ],
        compiler_params=pltpu.CompilerParams(
            collective_id=0, has_side_effects=True, vmem_limit_bytes=60 * 2**20
        ),
    )(images, first_weight, deep_weight.T, deep_cotangent)
    return first, deep.T


def solution(mesh):
    return jax.shard_map(
        on_device,
        mesh=mesh,
        in_specs=(P("sample", "row", "col"), P(), P(None, "col"), P("sample", "col", "row", None)),
        out_specs=(P(), P("row", "col")),
        check_vma=False,
    )
```

time: 51.2 us -> 41.6 us (0.81)
  Pallas kernels: 46.7 us -> 38.4 us
  local copies, waits for them, and re-layouts: 3.59 us -> 2.32 us
    pallas_call x1, Pallas kernels: 46.7 us -> 38.4 us  [on_device(): pl.pallas_call(kernel, out_shape=(jax.ShapeDtypeStruct((576, 128), F32),...]
    pallas_call x1 -> x0, local copies, waits for them, and re-layouts: 0.69 us -> none  [on_device(): pl.pallas_call(kernel, out_shape=(jax.ShapeDtypeStruct((576, 128), F32),...]
    unnamed x8 -> x4, local copies, waits for them, and re-layouts: 2.9 us -> 2.32 us
where the time goes in v2:
time: 41.6 us; the launch traced here: 41.4 us
  Pallas kernels  38.4 us (92%)
  local copies, waits for them, and re-layouts  2.32 us (6%)
  between operations  0.65 us (2%)
    pallas_call x1, Pallas kernels, on_device(): pl.pallas_call(kernel, out_shape=(jax.ShapeDtypeStruct((576, 128), F32),...  38.4 us
    unnamed x4, local copies, waits for them, and re-layouts  2.32 us

profile of v2, /device:TPU:1, one launch (start us, length us, event | category | flops | bytes accessed | tf_op | source)
XLA Modules:
  0.0 41.4 jit_solution(2974184487568163004)
XLA Ops:
  0.6 38.4 %shard_map.59 = (f32[576,128]{1,0:T(8,128)}, f32[32,144]{1,0:T(8,128)}) custom-call(bf16[1,64,4096]{2,1,0:T(8,128)(2,1)} %img.1, bf16[576,128]{1,0:T(8,128)(2,1)} %w1.1, bf16[32,1152]{1,0:T(8,128)(2,1)} %bitcast.2, bf16[1,32,16,128]{3,2,1,0:T(8,128)(2,1)} %cot.1), custom_call_target="tpu_custom_call" | custom-call | tf_op jit(solution)/shard_map/pallas_call | solution.py:436
  39.1 0.0 copy-start
  39.1 1.7 %copy.8 = f32[576,128]{1,0:T(8,128)} copy(f32[576,128]{1,0:T(8,128)} %get-tuple-element.8) | data formatting | bytes 589824
  40.8 0.0 copy-done
  40.8 0.6 %copy.9 = f32[144,32]{0,1:T(8,128)} copy(f32[144,32]{0,1:T(8,128)S(1)} %bitcast.3) | data formatting | bytes 36864
Async XLA Ops:
  39.1 1.7 %copy-start = (f32[32,144]{1,0:T(8,128)S(1)}, f32[32,144]{1,0:T(8,128)}, u32[]{:S(2)}) copy-start(f32[32,144]{1,0:T(8,128)} %get-tuple-element.5) | copy-start | bytes 55300

commit v3 on v2

--- a/solution.py
+++ b/solution.py
@@ -60,16 +60,15 @@
 
 
 def kernel(
-    img, w1, wd, cot, out1, out2,
+    img, w1, wd, cot, first_sum, deep_sum,
     xe, w1v, wdv, cotv, xr, w1f, wf, wdf, wt, cotf, cs, cr, q, acte, acto, sle, slo, patch,
-    gwt, pair_in, half, ra, gt, fa, sb, rb, sb2, rb2, gtall, o2,
+    gw, pair_in, half, ra, gt, fa, sb, rb, sb2, rb2, gtall,
     in_sem, halo_s, halo_r, w_s, w_r, v_s, v_r, c_s, c_r, d0_s, d0_r, d1_s, d1_r, d2_s, d2_r,
     f1_s, f1_r, f2_s, f2_r, f3_s, f3_r,
 ):
     s, r, c = (lax.axis_index(name) for name in ("sample", "row", "col"))
     core = lax.rem(r, 2)
     partner = r + 1 - 2 * core
-    group = s * N_ROW + r
     plane = s * N_COL + c
 
     inputs = [
@@ -82,9 +81,6 @@
     def in_plane(k, sign=1):
         return (lax.rem(s + k // N_COL, 2), lax.rem(c + N_COL + sign * (k % N_COL), N_COL))
 
-    def in_group(k, sign=1):
-        return (lax.rem(s + k // N_ROW, 2), lax.rem(r + N_ROW + sign * (k % N_ROW), N_ROW))
-
     down, right = lax.rem(r + 1, N_ROW), lax.rem(c + 1, N_COL)
     up, left = lax.rem(r + N_ROW - 1, N_ROW), lax.rem(c + N_COL - 1, N_COL)
 
@@ -93,10 +89,8 @@
     for k in range(1, N_BOTH):
         ps, pc = in_plane(k)
         greeted.append((ps, r, pc))
-    for k in range(1, N_BOTH):
-        if k != N_ROW:
-            ps, pr = in_group(k)
-            greeted.append((ps, pr, c))
+    for k in range(1, N_ROW):
+        greeted.append((s, lax.rem(r + k, N_ROW), c))
     for device in greeted:
         pl.semaphore_signal(barrier, inc=1, device_id=device, device_id_type=MESH)
     for copy in inputs:
@@ -249,8 +243,7 @@
         handed_on.pairs[k][0].start()
 
     cotangents.wait_recv()
-    lane = lax.broadcasted_iota(jnp.int32, (16, 128), 1)
-    quarter = lane // 32
+    quarter = lax.broadcasted_iota(jnp.int32, (16, 128), 1) // 32
     def from_col(col):
         return lax.rem(z + 4 - col // 2, 4) + 4 * lax.rem(xhi + col % 2, 2)
 
@@ -306,20 +299,20 @@
     first1 = Fan(first1)
     first1.start()
 
-    gwt[...] = tn(dg, patch[...]).astype(BF).reshape(8, 2, 16, 1152)
-    pair = remote(gwt.at[:, 1 - core], pair_in, d0_s.at[0], d0_r.at[0], (s, partner, c))
+    gw[...] = tn(patch[...], dg).astype(BF).reshape(9, 4, 2, 16, 256)
+    pair = remote(gw.at[:, :, 1 - core], pair_in, d0_s.at[0], d0_r.at[0], (s, partner, c))
     pair.start()
     pair.wait_recv()
-    half[...] = (gwt[:, core].astype(F32) + pair_in[...].astype(F32)).astype(BF)
-
+    half[...] = (gw[:, :, core].astype(F32) + pair_in[...].astype(F32)).astype(BF)
+
+    y = r // 2
     deep1 = []
-    for k, (dz, dx) in enumerate(far_first):
-        ps, pc = across(dz, dx)
-        qs, qc = across(dz, dx, -1)
+    for k in (2, 1, 3):
+        py, qy = lax.rem(y + k, 4), lax.rem(y + 4 - k, 4)
         deep1.append(
             (
-                remote(half.at[pc], ra.at[k], d1_s.at[k], d1_r.at[k], (ps, r, pc)),
-                remote(half.at[qc], ra.at[k], d1_s.at[k], d1_r.at[k], (qs, r, qc)),
+                remote(half.at[:, py], ra.at[k], d1_s.at[k], d1_r.at[k], (s, 2 * py + core, c)),
+                remote(half.at[:, qy], ra.at[k], d1_s.at[k], d1_r.at[k], (s, 2 * qy + core, c)),
             )
         )
     deep1 = Fan(deep1)
@@ -345,28 +338,29 @@
     rb2[plane] = sb2[...]
 
     deep1.wait_recv()
-    total = half[c].astype(F32)
-    for k in range(7):
+    total = half[:, y].astype(F32)
+    for k in range(1, 4):
         total = total + ra[k].astype(F32)
-    block = jnp.concatenate([total[:, 128 * tap : 128 * tap + 128] for tap in range(8)], 0)
-    sb[0] = nt(unit, block.astype(BF)).astype(BF)
-    block = jnp.concatenate([total[:, 1024:1152], jnp.zeros((112, 128), F32)], 0)
-    sb[1] = nt(unit, block.astype(BF)).astype(BF)
+    for h in range(2):
+        block = total[0:8, :, 128 * h : 128 * h + 128].reshape(128, 128)
+        sb[4 * h : 4 * h + 4, 0:2] = nt(unit, block.astype(BF)).astype(BF).reshape(4, 2, 16, 128)
+        last = total[8, :, 128 * h : 128 * h + 128]
+        for p in range(4):
+            moved = pltpu.roll(last, 128 - 32 * p, 1) if p else last
+            sb[4 * h + p, 2] = moved.astype(BF)
     deep2 = []
     for k in range(N_BOTH - 1, 0, -1):
-        ps, pr = in_group(k)
-        qs, qr = in_group(k, -1)
+        ps, pc = in_plane(k)
+        qs, qc = in_plane(k, -1)
         deep2.append(
             (
-                remote(sb.at[:, rows_of(pr, 16), :], rb.at[group], d2_s.at[k], d2_r.at[k], (ps, pr, c)),
-                remote(
-                    sb.at[:, rows_of(qr, 16), :], rb.at[qs * N_ROW + qr], d2_s.at[k], d2_r.at[k], (qs, qr, c)
-                ),
+                remote(sb.at[pc], rb.at[plane], d2_s.at[k], d2_r.at[k], (ps, r, pc)),
+                remote(sb.at[qc], rb.at[qs * N_COL + qc], d2_s.at[k], d2_r.at[k], (qs, r, qc)),
             )
         )
     deep2 = Fan(deep2)
     deep2.start()
-    rb[group] = sb[:, rows_of(r, 16), :]
+    rb[plane] = sb[c]
 
     first2.wait_recv()
     total = rb2[0].astype(F32)
@@ -386,48 +380,48 @@
     first3.start()
 
     deep2.wait_recv()
-    halves = []
-    for which in range(2):
-        total = rb[which].astype(F32)
-        for p in range(which + 2, N_BOTH, 2):
-            total = total + rb[p].astype(F32)
-        halves.append(total)
-    for tap in range(9):
-        lower, upper = (h[tap // 8] for h in halves)
-        shift = (128 - 16 * (tap % 8)) % 128
-        lower = pltpu.roll(lower, shift, 1) if shift else lower
-        upper = pltpu.roll(upper, (shift + 16) % 128, 1) if (shift + 16) % 128 else upper
-        o2[pl.ds(tap, 16, stride=9), :] = jnp.where(lane < 16, lower, upper)
-    out2[...] = o2[...].T[0:32, 0:144]
+    total = rb[0].astype(F32)
+    for p in range(1, N_BOTH):
+        total = total + rb[p].astype(F32)
+    deep_sum[...] = total
 
     first3.wait_recv()
+    first_sum[...] = gtall[...]
+
+    @pl.when(sends_down)
+    def _():
+        to_down.wait_send()
+
+    @pl.when(sends_right)
+    def _():
+        to_right.wait_send()
+
+    @pl.when(jnp.logical_and(sends_down, sends_right))
+    def _():
+        to_corner.wait_send()
+
+    pair.wait_send()
+    for fan in (weights, handed_on, cotangents, first1, deep1, first2, deep2, first3):
+        fan.wait_send()
+
+
+def finish(first_sum, deep_sum, out1, out2, o2):
+    unit = eye(128)
     places = ((0, 1), (0, 2), (1, 1), (1, 2), (2, 1), (2, 2), (1, 0), (0, 0), None, (2, 0))
     for j in range(5):
-        block = nt(unit, gtall[:, 128 * j : 128 * j + 128])
+        block = nt(unit, first_sum[:, 128 * j : 128 * j + 128])
         for i in range(2):
             place = places[2 * j + i]
             if place is not None:
                 out1[pl.ds(3 * place[0] + place[1], 64, stride=9), :] = block[64 * i : 64 * i + 64]
-
-    @pl.when(sends_down)
-    def _():
-        to_down.wait_send()
-
-    @pl.when(sends_right)
-    def _():
-        to_right.wait_send()
-
-    @pl.when(jnp.logical_and(sends_down, sends_right))
-    def _():
-        to_corner.wait_send()
-
-    pair.wait_send()
-    for fan in (weights, handed_on, cotangents, first1, deep1, first2, deep2, first3):
-        fan.wait_send()
+    most = jnp.concatenate([deep_sum[0], deep_sum[1], jnp.zeros((96, 128), F32)], 0).T
+    for tap in range(9):
+        o2[pl.ds(tap, 16, stride=9), :] = most[16 * tap : 16 * tap + 16] if tap < 8 else deep_sum[2]
+    out2[...] = o2[...].T[0:32, 0:144]
 
 
 def on_device(images, first_weight, deep_weight, deep_cotangent):
-    anywhere = pl.BlockSpec(memory_space=pl.ANY)
+    anywhere = pl.BlockSpec(memory_space=pltpu.HBM)
     vmem = pl.BlockSpec(memory_space=pltpu.VMEM)
 
     def dma(count):
@@ -435,7 +429,7 @@
 
     first, deep = pl.pallas_call(
         kernel,
-        out_shape=(jax.ShapeDtypeStruct((576, 128), F32), jax.ShapeDtypeStruct((32, 144), F32)),
+        out_shape=(jax.ShapeDtypeStruct((128, 640), BF), jax.ShapeDtypeStruct((3, 16, 128), F32)),
         in_specs=[anywhere] * 4,
         out_specs=(vmem, vmem),
         scratch_shapes=[
@@ -457,25 +451,32 @@
             pltpu.VMEM((3, 17, 16, 128), F32),
             pltpu.VMEM((3, 16, 16, 128), F32),
             pltpu.VMEM((256, 1152), BF),
-            pltpu.VMEM((8, 2, 16, 1152), BF),
-            pltpu.VMEM((8, 16, 1152), BF),
-            pltpu.VMEM((8, 16, 1152), BF),
-            pltpu.VMEM((7, 16, 1152), BF),
+            pltpu.VMEM((9, 4, 2, 16, 256), BF),
+            pltpu.VMEM((9, 4, 16, 256), BF),
+            pltpu.VMEM((9, 4, 16, 256), BF),
+            pltpu.VMEM((4, 9, 16, 256), BF),
             pltpu.VMEM((128, 640), BF),
             pltpu.VMEM((8, 16, 640), BF),
-            pltpu.VMEM((2, 128, 128), BF),
-            pltpu.VMEM((16, 2, 16, 128), BF),
+            pltpu.VMEM((8, 3, 16, 128), BF),
+            pltpu.VMEM((16, 3, 16, 128), BF),
             pltpu.VMEM((16, 640), BF),
             pltpu.VMEM((16, 16, 640), BF),
             pltpu.VMEM((128, 640), BF),
-            pltpu.VMEM((256, 128), F32),
             pltpu.SemaphoreType.DMA((4,)),
-            *dma(3), *dma(7), *dma(7), *dma(7), *dma(1), *dma(7), *dma(16), *dma(8), *dma(16), *dma(8),
+            *dma(3), *dma(7), *dma(7), *dma(7), *dma(1), *dma(4), *dma(16), *dma(8), *dma(16), *dma(8),
         ],
         compiler_params=pltpu.CompilerParams(
             collective_id=0, has_side_effects=True, vmem_limit_bytes=60 * 2**20
         ),
     )(images, first_weight, deep_weight.T, deep_cotangent)
+    first, deep = pl.pallas_call(
+        finish,
+        out_shape=(jax.ShapeDtypeStruct((576, 128), F32), jax.ShapeDtypeStruct((32, 144), F32)),
+        in_specs=[vmem, vmem],
+        out_specs=(vmem, vmem),
+        scratch_shapes=[pltpu.VMEM((256, 128), F32)],
+        compiler_params=pltpu.CompilerParams(vmem_limit_bytes=60 * 2**20),
+    )(first, deep)
     return first, deep.T
 
 

time: 41.6 us -> 40.5 us (0.974)
  local copies, waits for them, and re-layouts: 2.32 us -> 0 us
  Pallas kernels: 38.4 us -> 39.7 us
    unnamed x4 -> x0, local copies, waits for them, and re-layouts: 2.32 us -> none
    pallas_call x1 -> x2, Pallas kernels: 38.4 us -> 39.7 us  [the longest x1 37.9 us: on_device(): pl.pallas_call(kernel, out_shape=(jax.ShapeDtypeStruct((128, 640), BF), j...]
where the time goes in v3:
time: 40.5 us; the launch traced here: 40.4 us
  Pallas kernels  39.7 us (98%)
  between operations  0.64 us (2%)
    pallas_call x1, Pallas kernels, on_device(): pl.pallas_call(kernel, out_shape=(jax.ShapeDtypeStruct((128, 640), BF), j...  37.9 us
    pallas_call x1, Pallas kernels, on_device(): pl.pallas_call(finish, out_shape=(jax.ShapeDtypeStruct((576, 128), F32),...  1.88 us

profile of v3, /device:TPU:1, one launch (start us, length us, event | category | flops | bytes accessed | tf_op | source)
XLA Modules:
  0.0 40.4 jit_solution(752132363264178769)
XLA Ops:
  0.6 37.9 %shard_map.59 = (bf16[128,640]{1,0:T(8,128)(2,1)}, f32[3,16,128]{2,1,0:T(8,128)}) custom-call(bf16[1,64,4096]{2,1,0:T(8,128)(2,1)} %img.1, bf16[576,128]{1,0:T(8,128)(2,1)} %w1.1, bf16[32,1152]{1,0:T(8,128)(2,1)} %bitcast.2, bf16[1,32,16,128]{3,2,1,0:T(8,128)(2,1)} %cot.1), custom_call_target="tpu_custom_call" | custom-call | tf_op jit(solution)/shard_map/pallas_call | solution.py:430
  38.5 1.9 %shard_map.60 = (f32[576,128]{1,0:T(8,128)}, f32[32,144]{1,0:T(8,128)}) custom-call(bf16[128,640]{1,0:T(8,128)(2,1)} %get-tuple-element.6.first_sum, f32[3,16,128]{2,1,0:T(8,128)} %get-tuple-element.7.deep_sum), custom_call_target="tpu_custom_call" | custom-call | tf_op jit(solution)/shard_map/pallas_call | solution.py:472

commit v4 on v3

--- a/solution.py
+++ b/solution.py
@@ -9,6 +9,12 @@
 F32 = jnp.float32
 MESH = pl.DeviceIdType.MESH
 
+HOPS = {(0, 0): 0, (0, 1): 1, (1, 1): 1, (1, 0): 2}
+PLANE = sorted(
+    ((dz, fx, fs) for dz in range(4) for fx in range(2) for fs in range(2) if dz + fx + fs),
+    key=lambda step: -(min(step[0], 4 - step[0]) + HOPS[step[1:]]),
+)
+LINE = (4, 5, 3, 2, 6, 7, 1)
 N_ROW = 8
 N_COL = 8
 N_BOTH = 16
@@ -78,18 +84,21 @@
         pltpu.make_async_copy(img.at[0], xe.at[pl.ds(16, 64), pl.ds(256, 4096)], in_sem.at[3]),
     ]
 
-    def in_plane(k, sign=1):
-        return (lax.rem(s + k // N_COL, 2), lax.rem(c + N_COL + sign * (k % N_COL), N_COL))
+    z, xhi = c // 2, lax.rem(c, 2)
+
+    def in_plane(step, sign=1):
+        dz, fx, fs = step
+        return lax.rem(s + fs, 2), lax.rem(z + 4 + sign * dz, 4) * 2 + lax.rem(xhi + fx, 2)
 
     down, right = lax.rem(r + 1, N_ROW), lax.rem(c + 1, N_COL)
     up, left = lax.rem(r + N_ROW - 1, N_ROW), lax.rem(c + N_COL - 1, N_COL)
 
     barrier = pltpu.get_barrier_semaphore()
     greeted = [(s, down, right), (s, up, left)]
-    for k in range(1, N_BOTH):
-        ps, pc = in_plane(k)
+    for step in PLANE:
+        ps, pc = in_plane(step)
         greeted.append((ps, r, pc))
-    for k in range(1, N_ROW):
+    for k in LINE:
         greeted.append((s, lax.rem(r + k, N_ROW), c))
     for device in greeted:
         pl.semaphore_signal(barrier, inc=1, device_id=device, device_id_type=MESH)
@@ -141,10 +150,8 @@
     def _():
         to_right.start()
 
-    z, xhi = c // 2, lax.rem(c, 2)
-
     def across(dz, dx, sign=1):
-        return lax.rem(s + dx, 2), lax.rem(z + 4 + sign * dz, 4) * 2 + lax.rem(xhi + dx, 2)
+        return in_plane((dz, dx, dx), sign)
 
     def half_shard(col, which):
         return wt.at[pl.ds(pl.multiple_of(32 * col + 16 * which, 16), 16), :]
@@ -197,6 +204,10 @@
     @pl.when(jnp.logical_not(jnp.logical_and(has_up, has_left)))
     def _():
         xe[0:16, 0:256] = jnp.zeros((16, 256), BF)
+
+    for k in range(6, -1, -1):
+        weights.pairs[k][1].wait_recv()
+        handed_on.pairs[k][0].start()
 
     inputs[3].wait()
 
@@ -237,10 +248,6 @@
         patch[:, 384 * a : 384 * a + 128] = acte[a, 0:16].reshape(256, 128)
         patch[:, 384 * a + 128 : 384 * a + 256] = acto[a].reshape(256, 128)
         patch[:, 384 * a + 256 : 384 * a + 384] = acte[a, 1:17].reshape(256, 128)
-
-    for k in range(6, -1, -1):
-        weights.pairs[k][1].wait_recv()
-        handed_on.pairs[k][0].start()
 
     cotangents.wait_recv()
     quarter = lax.broadcasted_iota(jnp.int32, (16, 128), 1) // 32
@@ -288,7 +295,7 @@
     gt[:, 512:640] = totals[2][:, 0:128].astype(BF)
 
     first1 = []
-    for k in range(1, N_ROW):
+    for k in LINE:
         pr, qr = lax.rem(r + k, N_ROW), lax.rem(r + N_ROW - k, N_ROW)
         first1.append(
             (
@@ -324,9 +331,9 @@
         total = total + fa[k].astype(F32)
     sb2[...] = total.astype(BF)
     first2 = []
-    for k in range(N_BOTH - 1, 0, -1):
-        ps, pc = in_plane(k)
-        qs, qc = in_plane(k, -1)
+    for k, step in enumerate(PLANE):
+        ps, pc = in_plane(step)
+        qs, qc = in_plane(step, -1)
         first2.append(
             (
                 remote(sb2, rb2.at[plane], f2_s.at[k], f2_r.at[k], (ps, r, pc)),
@@ -349,9 +356,9 @@
             moved = pltpu.roll(last, 128 - 32 * p, 1) if p else last
             sb[4 * h + p, 2] = moved.astype(BF)
     deep2 = []
-    for k in range(N_BOTH - 1, 0, -1):
-        ps, pc = in_plane(k)
-        qs, qc = in_plane(k, -1)
+    for k, step in enumerate(PLANE):
+        ps, pc = in_plane(step)
+        qs, qc = in_plane(step, -1)
         deep2.append(
             (
                 remote(sb.at[pc], rb.at[plane], d2_s.at[k], d2_r.at[k], (ps, r, pc)),
@@ -368,7 +375,7 @@
         total = total + rb2[p].astype(F32)
     gtall[rows_of(r, 16), :] = total.astype(BF)
     first3 = []
-    for k in range(1, N_ROW):
+    for k in LINE:
         pr, qr = lax.rem(r + k, N_ROW), lax.rem(r + N_ROW - k, N_ROW)
         first3.append(
             (

time: 40.5 us -> 39 us (0.963)
  Pallas kernels: 39.7 us -> 38.2 us
    pallas_call x1, Pallas kernels: 37.9 us -> 36.3 us  [on_device(): pl.pallas_call(kernel, out_shape=(jax.ShapeDtypeStruct((128, 640), BF), j...]
where the time goes in v4:
time: 39 us; the launch traced here: 38.8 us
  Pallas kernels  38.2 us (98%)
  between operations  0.64 us (2%)
    pallas_call x1, Pallas kernels, on_device(): pl.pallas_call(kernel, out_shape=(jax.ShapeDtypeStruct((128, 640), BF), j...  36.3 us
    pallas_call x1, Pallas kernels, on_device(): pl.pallas_call(finish, out_shape=(jax.ShapeDtypeStruct((576, 128), F32),...  1.88 us

profile of v4, /device:TPU:1, one launch (start us, length us, event | category | flops | bytes accessed | tf_op | source)
XLA Modules:
  0.0 38.8 jit_solution(17889404132858366153)
XLA Ops:
  0.6 36.3 %shard_map.59 = (bf16[128,640]{1,0:T(8,128)(2,1)}, f32[3,16,128]{2,1,0:T(8,128)}) custom-call(bf16[1,64,4096]{2,1,0:T(8,128)(2,1)} %img.1, bf16[576,128]{1,0:T(8,128)(2,1)} %w1.1, bf16[32,1152]{1,0:T(8,128)(2,1)} %bitcast.2, bf16[1,32,16,128]{3,2,1,0:T(8,128)(2,1)} %cot.1), custom_call_target="tpu_custom_call" | custom-call | tf_op jit(solution)/shard_map/pallas_call | solution.py:437
  37.0 1.9 %shard_map.60 = (f32[576,128]{1,0:T(8,128)}, f32[32,144]{1,0:T(8,128)}) custom-call(bf16[128,640]{1,0:T(8,128)(2,1)} %get-tuple-element.6.first_sum, f32[3,16,128]{2,1,0:T(8,128)} %get-tuple-element.7.deep_sum), custom_call_target="tpu_custom_call" | custom-call | tf_op jit(solution)/shard_map/pallas_call | solution.py:479

commit v5 on v4

--- a/solution.py
+++ b/solution.py
@@ -473,16 +473,16 @@
             *dma(3), *dma(7), *dma(7), *dma(7), *dma(1), *dma(4), *dma(16), *dma(8), *dma(16), *dma(8),
         ],
         compiler_params=pltpu.CompilerParams(
-            collective_id=0, has_side_effects=True, vmem_limit_bytes=60 * 2**20
+            collective_id=0, has_side_effects=True, vmem_limit_bytes=40 * 2**20
         ),
-    )(images, first_weight, deep_weight.T, deep_cotangent)
+    )(*(pltpu.with_memory_space_constraint(v, pltpu.HBM) for v in (images, first_weight, deep_weight.T, deep_cotangent)))
     first, deep = pl.pallas_call(
         finish,
         out_shape=(jax.ShapeDtypeStruct((576, 128), F32), jax.ShapeDtypeStruct((32, 144), F32)),
         in_specs=[vmem, vmem],
         out_specs=(vmem, vmem),
         scratch_shapes=[pltpu.VMEM((256, 128), F32)],
-        compiler_params=pltpu.CompilerParams(vmem_limit_bytes=60 * 2**20),
+        compiler_params=pltpu.CompilerParams(vmem_limit_bytes=40 * 2**20),
     )(first, deep)
     return first, deep.T
 

time: 39 us -> 37.4 us (0.959)
  Pallas kernels: 38.2 us -> 36.6 us
    pallas_call x1, Pallas kernels: 1.88 us -> 0.96 us  [on_device(): pl.pallas_call(finish, out_shape=(jax.ShapeDtypeStruct((576, 128), F32),...]
    pallas_call x1, Pallas kernels: 36.3 us -> 35.7 us  [on_device(): pl.pallas_call(kernel, out_shape=(jax.ShapeDtypeStruct((128, 640), BF), j...]
where the time goes in v5:
time: 37.4 us; the launch traced here: 37.3 us
  Pallas kernels  36.6 us (98%)
  between operations  0.64 us (2%)
    pallas_call x1, Pallas kernels, on_device(): pl.pallas_call(kernel, out_shape=(jax.ShapeDtypeStruct((128, 640), BF), j...  35.7 us
    pallas_call x1, Pallas kernels, on_device(): pl.pallas_call(finish, out_shape=(jax.ShapeDtypeStruct((576, 128), F32),...  0.96 us

profile of v5, /device:TPU:1, one launch (start us, length us, event | category | flops | bytes accessed | tf_op | source)
XLA Modules:
  0.0 37.3 jit_solution(17743514615377797258)
XLA Ops:
  0.6 35.7 %shard_map.59 = (bf16[128,640]{1,0:T(8,128)(2,1)S(1)}, f32[3,16,128]{2,1,0:T(8,128)S(1)}) custom-call(bf16[1,64,4096]{2,1,0:T(8,128)(2,1)} %img.1, bf16[576,128]{1,0:T(8,128)(2,1)} %w1.1, bf16[32,1152]{1,0:T(8,128)(2,1)} %bitcast.2, bf16[1,32,16,128]{3,2,1,0:T(8,128)(2,1)} %cot.1), custom_call_target="tpu_custom_call" | custom-call | tf_op jit(solution)/shard_map/pallas_call | solution.py:437
  36.3 1.0 %shard_map.60 = (f32[576,128]{1,0:T(8,128)}, f32[32,144]{1,0:T(8,128)}) custom-call(bf16[128,640]{1,0:T(8,128)(2,1)S(1)} %get-tuple-element.6.first_sum, f32[3,16,128]{2,1,0:T(8,128)S(1)} %get-tuple-element.7.deep_sum), custom_call_target="tpu_custom_call" | custom-call | tf_op jit(solution)/shard_map/pallas_call | solution.py:479

commit v6 on v5

--- a/solution.py
+++ b/solution.py
@@ -91,10 +91,9 @@
         return lax.rem(s + fs, 2), lax.rem(z + 4 + sign * dz, 4) * 2 + lax.rem(xhi + fx, 2)
 
     down, right = lax.rem(r + 1, N_ROW), lax.rem(c + 1, N_COL)
-    up, left = lax.rem(r + N_ROW - 1, N_ROW), lax.rem(c + N_COL - 1, N_COL)
 
     barrier = pltpu.get_barrier_semaphore()
-    greeted = [(s, down, right), (s, up, left)]
+    greeted = []
     for step in PLANE:
         ps, pc = in_plane(step)
         greeted.append((ps, r, pc))
@@ -136,15 +135,9 @@
 
     to_down = halo(0, img.at[0, pl.ds(48, 16), :], xe.at[pl.ds(0, 16), pl.ds(256, 4096)], (s, down, c))
     to_right = halo(1, img.at[0, :, pl.ds(3840, 256)], xe.at[pl.ds(16, 64), pl.ds(0, 256)], (s, r, right))
-    to_corner = halo(
-        2, img.at[0, pl.ds(48, 16), pl.ds(3840, 256)], xe.at[pl.ds(0, 16), pl.ds(0, 256)], (s, down, right)
-    )
+    to_corner = halo(2, xe.at[pl.ds(64, 16), pl.ds(0, 256)], xe.at[pl.ds(0, 16), pl.ds(0, 256)], (s, down, c))
     sends_down, sends_right = r < N_ROW - 1, c < N_COL - 1
     has_up, has_left = r > 0, c > 0
-
-    @pl.when(jnp.logical_and(sends_down, sends_right))
-    def _():
-        to_corner.start()
 
     @pl.when(sends_right)
     def _():
@@ -205,30 +198,39 @@
     def _():
         xe[0:16, 0:256] = jnp.zeros((16, 256), BF)
 
+    inputs[3].wait()
+
+    @pl.when(has_up)
+    def _():
+        to_down.wait_recv()
+
+    row = lax.broadcasted_iota(jnp.int32, (112, 80), 0)
+    col = lax.broadcasted_iota(jnp.int32, (112, 80), 1)
+    pick = (col == 13 + 4 * (row % 16) + row // 16).astype(F32).astype(BF)
+
+    def select(t):
+        xr[:, t] = nn(pick, xe[:, 256 * t : 256 * t + 256]).astype(BF).reshape(7, 16, 256)
+
+    for t in range(1, 17):
+        select(t)
+
+    @pl.when(has_left)
+    def _():
+        to_right.wait_recv()
+
+    @pl.when(jnp.logical_and(sends_down, has_left))
+    def _():
+        to_corner.start()
+
     for k in range(6, -1, -1):
         weights.pairs[k][1].wait_recv()
         handed_on.pairs[k][0].start()
 
-    inputs[3].wait()
-
-    @pl.when(has_up)
-    def _():
-        to_down.wait_recv()
-
-    @pl.when(has_left)
-    def _():
-        to_right.wait_recv()
-
     @pl.when(jnp.logical_and(has_up, has_left))
     def _():
         to_corner.wait_recv()
 
-    row = lax.broadcasted_iota(jnp.int32, (112, 80), 0)
-    col = lax.broadcasted_iota(jnp.int32, (112, 80), 1)
-    pick = (col == 13 + 4 * (row % 16) + row // 16).astype(F32).astype(BF)
-    for t in range(17):
-        got = nn(pick, xe[:, 256 * t : 256 * t + 256]).astype(BF)
-        xr[:, t] = got.reshape(7, 16, 256)
+    select(0)
 
     def even_of(p):
         return xr[p].reshape(272, 256)
@@ -403,7 +405,7 @@
     def _():
         to_right.wait_send()
 
-    @pl.when(jnp.logical_and(sends_down, sends_right))
+    @pl.when(jnp.logical_and(sends_down, has_left))
     def _():
         to_corner.wait_send()
 

time: 37.4 us -> 36.7 us (0.981)
  Pallas kernels: 36.6 us -> 35.9 us
    pallas_call x1, Pallas kernels: 35.7 us -> 35 us  [on_device(): pl.pallas_call(kernel, out_shape=(jax.ShapeDtypeStruct((128, 640), BF), j...]
where the time goes in v6:
time: 36.7 us; the launch traced here: 36.6 us
  Pallas kernels  35.9 us (98%)
  between operations  0.64 us (2%)
    pallas_call x1, Pallas kernels, on_device(): pl.pallas_call(kernel, out_shape=(jax.ShapeDtypeStruct((128, 640), BF), j...  35 us
    pallas_call x1, Pallas kernels, on_device(): pl.pallas_call(finish, out_shape=(jax.ShapeDtypeStruct((576, 128), F32),...  0.96 us

profile of v6, /device:TPU:1, one launch (start us, length us, event | category | flops | bytes accessed | tf_op | source)
XLA Modules:
  0.0 36.6 jit_solution(2703167864808801815)
XLA Ops:
  0.6 35.0 %shard_map.59 = (bf16[128,640]{1,0:T(8,128)(2,1)S(1)}, f32[3,16,128]{2,1,0:T(8,128)S(1)}) custom-call(bf16[1,64,4096]{2,1,0:T(8,128)(2,1)} %img.1, bf16[576,128]{1,0:T(8,128)(2,1)} %w1.1, bf16[32,1152]{1,0:T(8,128)(2,1)} %bitcast.2, bf16[1,32,16,128]{3,2,1,0:T(8,128)(2,1)} %cot.1), custom_call_target="tpu_custom_call" | custom-call | tf_op jit(solution)/shard_map/pallas_call | solution.py:439
  35.6 1.0 %shard_map.60 = (f32[576,128]{1,0:T(8,128)}, f32[32,144]{1,0:T(8,128)}) custom-call(bf16[128,640]{1,0:T(8,128)(2,1)S(1)} %get-tuple-element.6.first_sum, f32[3,16,128]{2,1,0:T(8,128)S(1)} %get-tuple-element.7.deep_sum), custom_call_target="tpu_custom_call" | custom-call | tf_op jit(solution)/shard_map/pallas_call | solution.py:481

commit v7 on v6

--- a/solution.py
+++ b/solution.py
@@ -139,10 +139,6 @@
     sends_down, sends_right = r < N_ROW - 1, c < N_COL - 1
     has_up, has_left = r > 0, c > 0
 
-    @pl.when(sends_right)
-    def _():
-        to_right.start()
-
     def across(dz, dx, sign=1):
         return in_plane((dz, dx, dx), sign)
 
@@ -169,6 +165,10 @@
     weights, handed_on = Fan(weights), Fan(handed_on)
     weights.start()
 
+    @pl.when(sends_right)
+    def _():
+        to_right.start()
+
     @pl.when(sends_down)
     def _():
         to_down.start()
@@ -184,26 +184,26 @@
             )
         )
     cotangents = Fan(cotangents)
+
+    @pl.when(jnp.logical_not(has_up))
+    def _():
+        xe[0:16, 256:4352] = jnp.zeros((16, 4096), BF)
+
+    @pl.when(jnp.logical_not(has_left))
+    def _():
+        xe[16:80, 0:256] = jnp.zeros((64, 256), BF)
+
+    @pl.when(jnp.logical_not(jnp.logical_and(has_up, has_left)))
+    def _():
+        xe[0:16, 0:256] = jnp.zeros((16, 256), BF)
+
+    inputs[3].wait()
+
+    @pl.when(has_up)
+    def _():
+        to_down.wait_recv()
+
     cotangents.start()
-
-    @pl.when(jnp.logical_not(has_up))
-    def _():
-        xe[0:16, 256:4352] = jnp.zeros((16, 4096), BF)
-
-    @pl.when(jnp.logical_not(has_left))
-    def _():
-        xe[16:80, 0:256] = jnp.zeros((64, 256), BF)
-
-    @pl.when(jnp.logical_not(jnp.logical_and(has_up, has_left)))
-    def _():
-        xe[0:16, 0:256] = jnp.zeros((16, 256), BF)
-
-    inputs[3].wait()
-
-    @pl.when(has_up)
-    def _():
-        to_down.wait_recv()
-
     row = lax.broadcasted_iota(jnp.int32, (112, 80), 0)
     col = lax.broadcasted_iota(jnp.int32, (112, 80), 1)
     pick = (col == 13 + 4 * (row % 16) + row // 16).astype(F32).astype(BF)
@@ -371,6 +371,22 @@
     deep2.start()
     rb[plane] = sb[c]
 
+    @pl.when(sends_down)
+    def _():
+        to_down.wait_send()
+
+    @pl.when(sends_right)
+    def _():
+        to_right.wait_send()
+
+    @pl.when(jnp.logical_and(sends_down, has_left))
+    def _():
+        to_corner.wait_send()
+
+    pair.wait_send()
+    for fan in (weights, handed_on, cotangents, first1, deep1):
+        fan.wait_send()
+
     first2.wait_recv()
     total = rb2[0].astype(F32)
     for p in range(1, N_BOTH):
@@ -394,24 +410,12 @@
         total = total + rb[p].astype(F32)
     deep_sum[...] = total
 
+    for fan in (first2, deep2):
+        fan.wait_send()
     first3.wait_recv()
     first_sum[...] = gtall[...]
 
-    @pl.when(sends_down)
-    def _():
-        to_down.wait_send()
-
-    @pl.when(sends_right)
-    def _():
-        to_right.wait_send()
-
-    @pl.when(jnp.logical_and(sends_down, has_left))
-    def _():
-        to_corner.wait_send()
-
-    pair.wait_send()
-    for fan in (weights, handed_on, cotangents, first1, deep1, first2, deep2, first3):
-        fan.wait_send()
+    first3.wait_send()
 
 
 def finish(first_sum, deep_sum, out1, out2, o2):

time: 36.7 us -> 36.1 us (0.984)
  Pallas kernels: 35.9 us -> 35.3 us
    pallas_call x1, Pallas kernels: 35 us -> 34.3 us  [on_device(): pl.pallas_call(kernel, out_shape=(jax.ShapeDtypeStruct((128, 640), BF), j...]
where the time goes in v7:
time: 36.1 us; the launch traced here: 35.9 us
  Pallas kernels  35.3 us (98%)
  between operations  0.64 us (2%)
    pallas_call x1, Pallas kernels, on_device(): pl.pallas_call(kernel, out_shape=(jax.ShapeDtypeStruct((128, 640), BF), j...  34.3 us
    pallas_call x1, Pallas kernels, on_device(): pl.pallas_call(finish, out_shape=(jax.ShapeDtypeStruct((576, 128), F32),...  0.96 us

profile of v7, /device:TPU:1, one launch (start us, length us, event | category | flops | bytes accessed | tf_op | source)
XLA Modules:
  0.0 35.9 jit_solution(11470861445938491947)
XLA Ops:
  0.6 34.3 %shard_map.59 = (bf16[128,640]{1,0:T(8,128)(2,1)S(1)}, f32[3,16,128]{2,1,0:T(8,128)S(1)}) custom-call(bf16[1,64,4096]{2,1,0:T(8,128)(2,1)} %img.1, bf16[576,128]{1,0:T(8,128)(2,1)} %w1.1, bf16[32,1152]{1,0:T(8,128)(2,1)} %bitcast.2, bf16[1,32,16,128]{3,2,1,0:T(8,128)(2,1)} %cot.1), custom_call_target="tpu_custom_call" | custom-call | tf_op jit(solution)/shard_map/pallas_call | solution.py:443
  35.0 1.0 %shard_map.60 = (f32[576,128]{1,0:T(8,128)}, f32[32,144]{1,0:T(8,128)}) custom-call(bf16[128,640]{1,0:T(8,128)(2,1)S(1)} %get-tuple-element.6.first_sum, f32[3,16,128]{2,1,0:T(8,128)S(1)} %get-tuple-element.7.deep_sum), custom_call_target="tpu_custom_call" | custom-call | tf_op jit(solution)/shard_map/pallas_call | solution.py:485

commit v8 on v7

--- a/solution.py
+++ b/solution.py
@@ -68,7 +68,7 @@
 def kernel(
     img, w1, wd, cot, first_sum, deep_sum,
     xe, w1v, wdv, cotv, xr, w1f, wf, wdf, wt, cotf, cs, cr, q, acte, acto, sle, slo, patch,
-    gw, pair_in, half, ra, gt, fa, sb, rb, sb2, rb2, gtall,
+    gw, pair_in, half, ra, gt, fa, sb, rb, sb2, rb2, gtall, o2,
     in_sem, halo_s, halo_r, w_s, w_r, v_s, v_r, c_s, c_r, d0_s, d0_r, d1_s, d1_r, d2_s, d2_r,
     f1_s, f1_r, f2_s, f2_r, f3_s, f3_r,
 ):
@@ -279,6 +279,7 @@
     back = nn(dg, wt[...])
     empty = jnp.zeros((1, 16, 128), F32)
     totals = [jnp.zeros((128, 256), F32) for _ in range(3)]
+    edge = []
     for a in range(3):
         part = [back[:, 384 * a + 128 * b : 384 * a + 128 * b + 128].reshape(16, 16, 128) for b in range(3)]
         even = jnp.concatenate([part[0], empty], 0) + jnp.concatenate([empty, part[2]], 0)
@@ -287,8 +288,13 @@
             even, odd = even.astype(BF).astype(F32), odd.astype(BF).astype(F32)
         even = (even * sle[a]).reshape(272, 128).astype(BF)
         odd = (odd * slo[a]).reshape(256, 128).astype(BF)
+        edge.append(even[0:16])
         for ta in range(3):
-            totals[ta] += tn(even, even_of(2 * a + ta)) + tn(odd, odd_of(2 * a + ta))
+            inner = xr[2 * a + ta, 1:17].reshape(256, 256)
+            totals[ta] += tn(even[16:272], inner) + tn(odd, odd_of(2 * a + ta))
+    edge = jnp.concatenate(edge, 0)
+    for ta in range(3):
+        totals[ta] += tn(edge, jnp.concatenate([xr[2 * a + ta, 0] for a in range(3)], 0))
     for ta in range(3):
         gt[:, 128 * ta : 128 * ta + 128] = totals[ta][:, 128:256].astype(BF)
     low = lax.broadcasted_iota(jnp.int32, (128, 128), 1) < 64
@@ -325,7 +331,6 @@
             )
         )
     deep1 = Fan(deep1)
-    deep1.start()
 
     first1.wait_recv()
     total = gt[rows_of(r, 16), :].astype(F32)
@@ -344,6 +349,7 @@
         )
     first2 = Fan(first2)
     first2.start()
+    deep1.start()
     rb2[plane] = sb2[...]
 
     deep1.wait_recv()
@@ -408,7 +414,10 @@
     total = rb[0].astype(F32)
     for p in range(1, N_BOTH):
         total = total + rb[p].astype(F32)
-    deep_sum[...] = total
+    most = jnp.concatenate([total[0], total[1], jnp.zeros((96, 128), F32)], 0).T
+    for tap in range(9):
+        o2[pl.ds(tap, 16, stride=9), :] = most[16 * tap : 16 * tap + 16] if tap < 8 else total[2]
+    deep_sum[...] = o2[...].T[0:32, 0:144]
 
     for fan in (first2, deep2):
         fan.wait_send()
@@ -418,7 +427,7 @@
     first3.wait_send()
 
 
-def finish(first_sum, deep_sum, out1, out2, o2):
+def finish(first_sum, deep_sum, out1, out2):
     unit = eye(128)
     places = ((0, 1), (0, 2), (1, 1), (1, 2), (2, 1), (2, 2), (1, 0), (0, 0), None, (2, 0))
     for j in range(5):
@@ -427,10 +436,7 @@
             place = places[2 * j + i]
             if place is not None:
                 out1[pl.ds(3 * place[0] + place[1], 64, stride=9), :] = block[64 * i : 64 * i + 64]
-    most = jnp.concatenate([deep_sum[0], deep_sum[1], jnp.zeros((96, 128), F32)], 0).T
-    for tap in range(9):
-        o2[pl.ds(tap, 16, stride=9), :] = most[16 * tap : 16 * tap + 16] if tap < 8 else deep_sum[2]
-    out2[...] = o2[...].T[0:32, 0:144]
+    out2[...] = deep_sum[...]
 
 
 def on_device(images, first_weight, deep_weight, deep_cotangent):
@@ -442,7 +448,7 @@
 
     first, deep = pl.pallas_call(
         kernel,
-        out_shape=(jax.ShapeDtypeStruct((128, 640), BF), jax.ShapeDtypeStruct((3, 16, 128), F32)),
+        out_shape=(jax.ShapeDtypeStruct((128, 640), BF), jax.ShapeDtypeStruct((32, 144), F32)),
         in_specs=[anywhere] * 4,
         out_specs=(vmem, vmem),
         scratch_shapes=[
@@ -475,6 +481,7 @@
             pltpu.VMEM((16, 640), BF),
             pltpu.VMEM((16, 16, 640), BF),
             pltpu.VMEM((128, 640), BF),
+            pltpu.VMEM((256, 128), F32),
             pltpu.SemaphoreType.DMA((4,)),
             *dma(3), *dma(7), *dma(7), *dma(7), *dma(1), *dma(4), *dma(16), *dma(8), *dma(16), *dma(8),
         ],
@@ -487,7 +494,6 @@
         out_shape=(jax.ShapeDtypeStruct((576, 128), F32), jax.ShapeDtypeStruct((32, 144), F32)),
         in_specs=[vmem, vmem],
         out_specs=(vmem, vmem),
-        scratch_shapes=[pltpu.VMEM((256, 128), F32)],
         compiler_params=pltpu.CompilerParams(vmem_limit_bytes=40 * 2**20),
     )(first, deep)
     return first, deep.T

time: 36.1 us -> 35.9 us (level)
  no operation moved by 1% of the time
where the time goes in v8:
time: 35.9 us; the launch traced here: 35.8 us
  Pallas kernels  35.2 us (98%)
  between operations  0.64 us (2%)
    pallas_call x1, Pallas kernels, on_device(): pl.pallas_call(kernel, out_shape=(jax.ShapeDtypeStruct((128, 640), BF), j...  34.2 us
    pallas_call x1, Pallas kernels, on_device(): pl.pallas_call(finish, out_shape=(jax.ShapeDtypeStruct((576, 128), F32),...  0.96 us

profile of v8, /device:TPU:1, one launch (start us, length us, event | category | flops | bytes accessed | tf_op | source)
XLA Modules:
  0.0 35.8 jit_solution(10458749891770589159)
XLA Ops:
  0.6 34.2 %shard_map.59 = (bf16[128,640]{1,0:T(8,128)(2,1)S(1)}, f32[32,144]{1,0:T(8,128)S(1)}) custom-call(bf16[1,64,4096]{2,1,0:T(8,128)(2,1)} %img.1, bf16[576,128]{1,0:T(8,128)(2,1)} %w1.1, bf16[32,1152]{1,0:T(8,128)(2,1)} %bitcast.2, bf16[1,32,16,128]{3,2,1,0:T(8,128)(2,1)} %cot.1), custom_call_target="tpu_custom_call" | custom-call | tf_op jit(solution)/shard_map/pallas_call | solution.py:449
  34.8 1.0 %shard_map.60 = (f32[576,128]{1,0:T(8,128)}, f32[32,144]{1,0:T(8,128)}) custom-call(bf16[128,640]{1,0:T(8,128)(2,1)S(1)} %get-tuple-element.6.first_sum, f32[32,144]{1,0:T(8,128)S(1)} %get-tuple-element.7.deep_sum), custom_call_target="tpu_custom_call" | custom-call | tf_op jit(solution)/shard_map/pallas_call | solution.py:492

commit v9 on v8

--- a/solution.py
+++ b/solution.py
@@ -68,7 +68,7 @@
 def kernel(
     img, w1, wd, cot, first_sum, deep_sum,
     xe, w1v, wdv, cotv, xr, w1f, wf, wdf, wt, cotf, cs, cr, q, acte, acto, sle, slo, patch,
-    gw, pair_in, half, ra, gt, fa, sb, rb, sb2, rb2, gtall, o2,
+    gw, pair_in, half, ra, gt, fa, sb, rb, sb2, rb2, o2,
     in_sem, halo_s, halo_r, w_s, w_r, v_s, v_r, c_s, c_r, d0_s, d0_r, d1_s, d1_r, d2_s, d2_r,
     f1_s, f1_r, f2_s, f2_r, f3_s, f3_r,
 ):
@@ -397,14 +397,14 @@
     total = rb2[0].astype(F32)
     for p in range(1, N_BOTH):
         total = total + rb2[p].astype(F32)
-    gtall[rows_of(r, 16), :] = total.astype(BF)
+    first_sum[rows_of(r, 16), :] = total.astype(BF)
     first3 = []
     for k in LINE:
         pr, qr = lax.rem(r + k, N_ROW), lax.rem(r + N_ROW - k, N_ROW)
         first3.append(
             (
-                remote(gtall.at[rows_of(r, 16), :], gtall.at[rows_of(r, 16), :], f3_s.at[k], f3_r.at[k], (s, pr, c)),
-                remote(gtall.at[rows_of(qr, 16), :], gtall.at[rows_of(qr, 16), :], f3_s.at[k], f3_r.at[k], (s, qr, c)),
+                remote(first_sum.at[rows_of(r, 16), :], first_sum.at[rows_of(r, 16), :], f3_s.at[k], f3_r.at[k], (s, pr, c)),
+                remote(first_sum.at[rows_of(qr, 16), :], first_sum.at[rows_of(qr, 16), :], f3_s.at[k], f3_r.at[k], (s, qr, c)),
             )
         )
     first3 = Fan(first3)
@@ -422,7 +422,6 @@
     for fan in (first2, deep2):
         fan.wait_send()
     first3.wait_recv()
-    first_sum[...] = gtall[...]
 
     first3.wait_send()
 
@@ -480,7 +479,6 @@
             pltpu.VMEM((16, 3, 16, 128), BF),
             pltpu.VMEM((16, 640), BF),
             pltpu.VMEM((16, 16, 640), BF),
-            pltpu.VMEM((128, 640), BF),
             pltpu.VMEM((256, 128), F32),
             pltpu.SemaphoreType.DMA((4,)),
             *dma(3), *dma(7), *dma(7), *dma(7), *dma(1), *dma(4), *dma(16), *dma(8), *dma(16), *dma(8),

time: 35.9 us -> 35.9 us (level)
  no operation moved by 1% of the time
where the time goes in v9:
time: 35.9 us; the launch traced here: 35.8 us
  Pallas kernels  35.1 us (98%)
  between operations  0.64 us (2%)
    pallas_call x1, Pallas kernels, on_device(): pl.pallas_call(kernel, out_shape=(jax.ShapeDtypeStruct((128, 640), BF), j...  34.2 us
    pallas_call x1, Pallas kernels, on_device(): pl.pallas_call(finish, out_shape=(jax.ShapeDtypeStruct((576, 128), F32),...  0.96 us

profile of v9, /device:TPU:1, one launch (start us, length us, event | category | flops | bytes accessed | tf_op | source)
XLA Modules:
  0.0 35.8 jit_solution(14397119032684291324)
XLA Ops:
  0.6 34.2 %shard_map.59 = (bf16[128,640]{1,0:T(8,128)(2,1)S(1)}, f32[32,144]{1,0:T(8,128)S(1)}) custom-call(bf16[1,64,4096]{2,1,0:T(8,128)(2,1)} %img.1, bf16[576,128]{1,0:T(8,128)(2,1)} %w1.1, bf16[32,1152]{1,0:T(8,128)(2,1)} %bitcast.2, bf16[1,32,16,128]{3,2,1,0:T(8,128)(2,1)} %cot.1), custom_call_target="tpu_custom_call" | custom-call | tf_op jit(solution)/shard_map/pallas_call | solution.py:448
  34.8 1.0 %shard_map.60 = (f32[576,128]{1,0:T(8,128)}, f32[32,144]{1,0:T(8,128)}) custom-call(bf16[128,640]{1,0:T(8,128)(2,1)S(1)} %get-tuple-element.6.first_sum, f32[32,144]{1,0:T(8,128)S(1)} %get-tuple-element.7.deep_sum), custom_call_target="tpu_custom_call" | custom-call | tf_op jit(solution)/shard_map/pallas_call | solution.py:490
